TPU v7x, 256 devices: a whole 4x4x8 slice. The times are simulated.
256 devices in a mesh: seq: 16 (over y_lo, x, core), head: 16 (over y_hi, z).
Axes of the slice: x: 4, y: 4 (y_hi: 2, y_lo: 2; y = y_hi * 2 + y_lo), z: 8, core: 2. Of those that a mesh axis runs over, the one named last changes fastest.
Arguments:
- queries: bfloat16 [2048, 8192], P('seq', 'head'), may hold values from -16 to 16
- cache_keys: bfloat16 [32768, 1024], P('seq'), may hold values from -16 to 16
- cache_values: bfloat16 [32768, 1024], P('seq'), may hold values from -6 to 6
- new_keys: bfloat16 [2048, 1024], P('seq'), may hold values from -6 to 6
- new_values: bfloat16 [2048, 1024], P('seq'), may hold values from -6 to 6
- out_weight: bfloat16 [8192, 8192], P('seq', 'head'), may hold values from -0.0625 to 0.0625
Outputs:
- mixed: bfloat16 [2048, 8192], P('seq', 'head')
All inputs are finite; a program needn't handle non-finite values.
Results may differ from a plain program's by a relative error of at most 0.028.
Values may be sent and summed in bfloat16 or wider, within the bound.
A program may use at most 128 MiB of HBM per device.

v0:
```python
import jax
import jax.numpy as jnp
from jax import lax
from jax.sharding import PartitionSpec as P

HQ = 64
KV = 8
HD = 128


def split_heads(rows, kv_local, g_local):
    return rows.reshape(rows.shape[0], kv_local, g_local, HD).transpose(1, 2, 0, 3)


def attend(carry_state, query_heads, query_pos, key_rows, value_rows, source, pre_rows, ch_rows):
    kv_local = query_heads.shape[0]
    key_heads = key_rows.reshape(-1, kv_local, HD).transpose(1, 0, 2)
    value_heads = value_rows.reshape(-1, kv_local, HD).transpose(1, 0, 2)
    key_pos = jnp.concatenate(
        [
            jnp.full((pre_rows,), -1, jnp.int32),
            source * ch_rows + jnp.arange(ch_rows, dtype=jnp.int32),
        ]
    )
    visible = key_pos[None, :] <= query_pos[:, None]
    scores = jnp.einsum(
        "kgqd,kld->kgql", query_heads, key_heads, preferred_element_type=jnp.float32
    ) * HD ** (-0.5)
    scores = jnp.where(visible, scores, -1e30)
    top_old, sum_old, summed_old = carry_state
    top_new = jnp.maximum(top_old, jnp.max(scores, axis=-1))
    weights = jnp.where(visible, jnp.exp(scores - top_new[..., None]), 0.0)
    factor = jnp.exp(top_old - top_new)
    weight_sum = sum_old * factor + jnp.sum(weights, axis=-1)
    summed = summed_old * factor[..., None] + jnp.einsum(
        "kgql,kld->kgqd",
        weights.astype(jnp.bfloat16),
        value_heads,
        preferred_element_type=jnp.float32,
    )
    return (top_new, weight_sum, summed)


def local(queries, cache_keys, cache_values, new_keys, new_values, out_weight):
    seq_index = lax.axis_index("seq")
    head_index = lax.axis_index("head")
    ch_rows = queries.shape[0]
    pre_rows = cache_keys.shape[0]
    key_span = pre_rows + ch_rows
    q_heads = queries.shape[1] // HD
    group_size = HQ // KV
    kv_local = max(1, q_heads // group_size)
    g_local = q_heads // kv_local
    kv_first = head_index * q_heads // group_size
    kv_width = kv_local * HD

    def kv_slice(matrix):
        return lax.dynamic_slice_in_dim(matrix, kv_first * HD, kv_width, 1)

    own_keys = jnp.concatenate([kv_slice(cache_keys), kv_slice(new_keys)], 0)
    own_values = jnp.concatenate([kv_slice(cache_values), kv_slice(new_values)], 0)
    initial = (
        jnp.full((kv_local, g_local, ch_rows), -1e30, jnp.float32),
        jnp.zeros((kv_local, g_local, ch_rows), jnp.float32),
        jnp.zeros((kv_local, g_local, ch_rows, HD), jnp.float32),
    )
    query_heads = split_heads(queries, kv_local, g_local)
    query_pos = seq_index * ch_rows + jnp.arange(ch_rows, dtype=jnp.int32)
    key_rows = lax.all_gather(own_keys, "seq", axis=0, tiled=True)
    value_rows = lax.all_gather(own_values, "seq", axis=0, tiled=True)
    shard_count = key_rows.shape[0] // key_span
    key_stack = key_rows.reshape(shard_count, key_span, kv_width)
    value_stack = value_rows.reshape(shard_count, key_span, kv_width)

    def one_shard(running, inputs):
        key_block, value_block, source = inputs
        return (
            attend(
                running, query_heads, query_pos, key_block, value_block, source, pre_rows, ch_rows
            ),
            None,
        )

    sources = jnp.arange(shard_count, dtype=jnp.int32)
    result, unused = lax.scan(one_shard, initial, (key_stack, value_stack, sources))
    top_final, weight_sum, summed = result
    attended = (summed / weight_sum[..., None]).astype(jnp.bfloat16)
    attended = attended.transpose(2, 0, 1, 3).reshape(ch_rows, q_heads * HD)
    gathered = lax.all_gather(attended, "head", axis=1, tiled=True)
    mixed = jnp.dot(
        gathered,
        lax.all_gather(out_weight, "seq", axis=0, tiled=True),
        preferred_element_type=jnp.float32,
    )
    return mixed.astype(jnp.bfloat16)


def solution(mesh):
    placed = (
        P("seq", "head"),
        P("seq", None),
        P("seq", None),
        P("seq", None),
        P("seq", None),
        P("seq", "head"),
    )
    return jax.shard_map(
        local, mesh=mesh, in_specs=placed, out_specs=P("seq", "head"), check_vma=False
    )
```

profile of v0, /device:TPU:6, one launch (start us, length us, event | category | flops | bytes accessed | tf_op | source)
XLA Modules:
  0.0 406.1 jit_solution(8141418016178086057)
XLA Ops:
  6.5 1.1 constant_dynamic-slice_fusion.1
  7.7 0.8 pad_maximum_fusion.1
  9.4 1.1 constant_dynamic-slice_fusion.3
  10.5 0.9 pad_maximum_fusion
  12.5 56.7 %all-gather.7.cloned.1.call-done = bf16[34816,128]{1,0:T(8,128)(2,1)} async-done(((bf16[2176,128]{1,0:T(8,128)(2,1)}), bf16[34816,128]{1,0:T(8,128)(2,1)}) %all-gather.7.cloned.1.call-update) | async-done | bytes 8912912 | tf_op jit(solution)/shard_map/all_gather | solution.py:70
  69.2 59.9 %all-gather.5.cloned.1.call-done = bf16[34816,128]{1,0:T(8,128)(2,1)} async-done(((bf16[2176,128]{1,0:T(8,128)(2,1)}), bf16[34816,128]{1,0:T(8,128)(2,1)}) %all-gather.5.cloned.1.call-update) | async-done | bytes 8912912 | tf_op jit(solution)/shard_map/all_gather | solution.py:69
  129.1 177.0 %while.15 = (s32[]{:T(128)}, f32[1,4,128]{2,1,0:T(4,128)S(1)}, f32[1,4,128]{2,1,0:T(4,128)S(1)}, f32[1,4,128,128]{3,2,1,0:T(8,128)S(1)}, s32[16]{0:T(128)S(1)}, ...) while((s32[]{:T(128)}, f32[1,4,128]{2,1,0:T(4,128)S(1)}, ...), condition=%wide.region_3.4_spmd.clone, body=%wide.region_0.3_spmd.clone.sunk | while | flops 580930816 | bytes 34132168 | solution.py:85
  130.4 1.0 broadcast_compare_fusion.2
  131.5 4.0 fusion.37
  135.4 3.8 fusion.40
  139.3 0.8 fusion.39
  141.5 1.0 broadcast_compare_fusion.2
  142.5 4.0 fusion.37
  146.5 3.9 fusion.40
  150.4 0.8 fusion.39
  152.6 1.0 broadcast_compare_fusion.2
  153.6 4.0 fusion.37
  157.6 3.9 fusion.40
  161.6 0.8 fusion.39
  163.7 1.0 broadcast_compare_fusion.2
  164.8 4.0 fusion.37
  168.8 3.9 fusion.40
  174.9 1.0 broadcast_compare_fusion.2
  175.9 4.0 fusion.37
  179.9 3.9 fusion.40
  183.8 0.8 fusion.39
  186.0 1.0 broadcast_compare_fusion.2
  187.0 4.0 fusion.37
  191.0 3.8 fusion.40
  194.9 0.8 fusion.39
  197.0 1.0 broadcast_compare_fusion.2
  198.1 4.0 fusion.37
  202.1 3.8 fusion.40
  205.9 0.8 fusion.39
  208.1 1.0 broadcast_compare_fusion.2
  209.1 4.0 fusion.37
  213.1 3.8 fusion.40
  217.0 0.8 fusion.39
  219.1 1.0 broadcast_compare_fusion.2
  220.2 4.0 fusion.37
  224.1 3.8 fusion.40
  230.2 1.0 broadcast_compare_fusion.2
  231.2 4.0 fusion.37
  235.2 3.8 fusion.40
  241.2 1.0 broadcast_compare_fusion.2
  242.2 4.0 fusion.37
  246.2 3.8 fusion.40
  252.2 1.0 broadcast_compare_fusion.2
  253.3 4.0 fusion.37
  257.3 3.8 fusion.40
  263.3 1.0 broadcast_compare_fusion.2
  264.3 4.0 fusion.37
  268.3 3.8 fusion.40
  274.3 1.0 broadcast_compare_fusion.2
  275.4 4.0 fusion.37
  279.3 3.8 fusion.40
  285.4 1.0 broadcast_compare_fusion.2
  286.4 4.0 fusion.37
  290.4 3.8 fusion.40
  296.4 1.0 broadcast_compare_fusion.2
  297.4 4.0 fusion.37
  301.4 3.8 fusion.40
  307.0 86.6 %all-gather.9.cloned.1.call-done = bf16[128,8192]{0,1:T(8,128)(2,1)} async-done(((bf16[128,512]{0,1:T(8,128)(2,1)}), bf16[128,8192]{0,1:T(8,128)(2,1)}) %all-gather.9.cloned.1.call-update) | async-done | bytes 2097168 | tf_op jit(solution)/shard_map/all_gather | solution.py:89
  393.6 6.0 %convolution_convert_fusion = bf16[128,512]{1,0:T(8,128)(2,1)} fusion(bf16[128,8192]{0,1:T(8,128)(2,1)} %all-gather.9.cloned.1.call-done, bf16[8192,512]{1,0:T(8,128)(2,1)} %all-gather.11.cloned.1.call-done), kind=kOutput, calls=%fused_computation.30 | convolution fusion | flops 1073807360 | bytes 10616832 | tf_op jit(solution)/shard_map/dot_general | solution.py:90
  (176 shorter events, 21.1 us)
Async XLA Ops:
  6.5 1.1 copy-start
  6.5 5.7 %copy-start.2 = (bf16[128,512]{1,0:T(8,128)(2,1)S(1)}, bf16[128,512]{1,0:T(8,128)(2,1)}, u32[]{:S(2)}) copy-start(bf16[128,512]{1,0:T(8,128)(2,1)} %param.8) | copy-start | bytes 393220
  6.5 62.7 %all-gather.7.cloned.1.call-start = ((), (), s32[]{:S(2)}) async-start(), calls=%async_computation.1 | async-start | bytes 9469952 | tf_op jit(solution)/shard_map/all_gather | solution.py:70
  8.6 120.5 %all-gather.5.cloned.1.call-start = ((), (), s32[]{:S(2)}) async-start(), calls=%async_computation | async-start | bytes 9469952 | tf_op jit(solution)/shard_map/all_gather | solution.py:69
  11.4 295.6 %all-gather.11.cloned.1.call-start = ((), (), s32[]{:S(2)}) async-start(), calls=%async_computation.3 | async-start | bytes 8912896 | tf_op jit(solution)/shard_map/all_gather | solution.py:92
  12.1 381.5 %all-gather.9.cloned.1.call-start = ((), (), s32[]{:S(2)}) async-start(), calls=%async_computation.2 | async-start | bytes 2228224 | tf_op jit(solution)/shard_map/all_gather | solution.py:89
  135.4 3.8 copy-start.1
  146.5 3.9 copy-start.1
  157.6 4.0 copy-start.1
  168.8 4.0 copy-start.1
  179.9 3.9 copy-start.1
  191.0 3.8 copy-start.1
  202.1 3.8 copy-start.1
  213.1 3.8 copy-start.1
  224.1 3.8 copy-start.1
  235.2 3.8 copy-start.1
  246.2 3.8 copy-start.1
  257.3 3.8 copy-start.1
  268.3 3.8 copy-start.1
  279.3 3.8 copy-start.1
  290.4 3.8 copy-start.1
  301.4 3.8 copy-start.1
Sparse Core Ops, SparseCore 0:
  9.2 59.9 all-gather.6
  71.0 58.0 all-gather.4
  131.0 55.5 all-gather.10
  307.1 86.4 all-gather.8
where the time goes:
time: 407 us; the launch traced here: 406 us
  waiting for transfers between devices  204 us (50%)
  matrix products  131 us (32%)
  other arithmetic  32.6 us (8%)
  local copies, waits for them, and re-layouts  13.8 us (3%)
  between operations  13.2 us (3%)
  loops' own time  11.2 us (3%)
    all_gather x1, waiting for transfers between devices, local(): gathered = lax.all_gather(attended, 'head', axis=1, tiled=True)  86.6 us
    dot_general x16, matrix products, attend(): jnp.einsum('kgqd,kld->kgql', query_heads, key_heads, preferred_element_ty...  63.5 us
    dot_general x16, matrix products, attend(): jnp.einsum('kgql,kld->kgqd', weights.astype(jnp.bfloat16), value_heads, p...  61.6 us
    all_gather x1, waiting for transfers between devices, local(): key_rows = lax.all_gather(own_keys, 'seq', axis=0, tiled=True)  59.9 us
    all_gather x1, waiting for transfers between devices, local(): value_rows = lax.all_gather(own_values, 'seq', axis=0, tiled=True)  56.7 us
    le x16, other arithmetic, attend(): visible = key_pos[None, :] <= query_pos[:, None]  16.6 us
    reduce_sum x16, other arithmetic, attend(): weight_sum = sum_old * factor + jnp.sum(weights, axis=-1)  13.1 us
    another operation x1, loops' own time, local(): lax.scan(one_shard, initial, (key_stack, value_stack, sources))  11.2 us
  transfers between devices with their start and end apart: 4, of which 3 were waited for; matrix products, arithmetic and copies ran while one was open for 42% of the time, Pallas kernels for 0%

commit v1 on v0

v1 whole, which is shorter than its diff:
```python
import functools

import jax
import jax.numpy as jnp
import numpy as np
from jax import lax
from jax.experimental import pallas as pl
from jax.experimental.pallas import tpu as pltpu
from jax.sharding import PartitionSpec as P

HD = 128
G = 4
COLS = G * 128
SHARD = 2048
CACHED = 2 * SHARD
KEYS = CACHED + 256
TK = 256
VR = 144
SCALE = float(HD**-0.5 * np.log2(np.e))
MESH = pl.DeviceIdType.MESH
F32, BF16 = jnp.float32, jnp.bfloat16


def kernel(
    q_ref, ck_ref, cv_ref, nk_ref, nv_ref, w_ref, out_ref,
    k2, vraw, vt, sbuf, qbuf, qt, osend, ssend, obuf, stbuf, abuf, wbuf, acc, csend, cbuf,
    loc_sem, kv_send, kv_recv, q_send, q_recv, w_send, w_recv, wf_send,
    o_send, o_recv, st_send, st_recv, a_send, a_recv, c_send, c_recv,
):
    s = lax.axis_index("seq")
    h = lax.axis_index("head")
    yl, x, c = s // 8, (s // 2) % 4, s % 2
    yh, z = h // 8, h % 8
    me_block = yl * 4 + x
    partner = (s + 1 - 2 * c, h)
    self_combine = yl == yh

    def seq_of(a, b):
        return a * 8 + b * 2 + c

    def item(i):
        step = i // 2
        gray = jnp.where(step == 2, 3, jnp.where(step == 3, 2, step))
        return (yl + i) % 2, (x + gray) % 4

    def remote(src, dst, ssem, rsem, dev):
        return pltpu.make_async_remote_copy(
            src_ref=src, dst_ref=dst, send_sem=ssem, recv_sem=rsem, device_id=dev, device_id_type=MESH
        )

    def arrived(ref, sem):
        pltpu.make_async_copy(ref, ref, sem).wait()

    kv_col = pl.ds(pl.multiple_of((h // 2) * HD, HD), HD)

    def cached_rows(core):
        return pl.ds(pl.multiple_of(core * SHARD, SHARD), SHARD)

    def new_rows(core):
        return pl.ds(pl.multiple_of(CACHED + core * 128, 128), 128)

    def kv_parts(core):
        return [
            (ck_ref.at[:, kv_col], k2.at[cached_rows(core), pl.ds(0, HD)]),
            (ck_ref.at[:, kv_col], k2.at[cached_rows(core), pl.ds(HD, HD)]),
            (nk_ref.at[:, kv_col], k2.at[new_rows(core), pl.ds(0, HD)]),
            (nk_ref.at[:, kv_col], k2.at[new_rows(core), pl.ds(HD, HD)]),
            (cv_ref.at[:, kv_col], vraw.at[cached_rows(core), :]),
            (nv_ref.at[:, kv_col], vraw.at[new_rows(core), :]),
        ]

    local = [
        pltpu.make_async_copy(src, dst, loc_sem.at[n]) for n, (src, dst) in enumerate(kv_parts(c))
    ]
    local.append(pltpu.make_async_copy(w_ref, wbuf.at[x * 2 + c], loc_sem.at[6]))
    local.append(pltpu.make_async_copy(q_ref, qbuf.at[me_block], loc_sem.at[7]))
    for copy in local:
        copy.start()

    barrier = pltpu.get_barrier_semaphore()

    def greet(dev):
        pl.semaphore_signal(barrier, inc=1, device_id=dev, device_id_type=MESH)

    for i in range(1, 8):
        b0, b1 = item(i)
        greet((seq_of(b0, b1), h))
    greet(partner)
    greet((s, yh * 8 + (z + 1) % 8))
    greet((s, yh * 8 + (z + 7) % 8))
    greet((s, (1 - yh) * 8 + z))
    for i in range(8):
        b0, b1 = item(i)
        if i == 0:
            @pl.when(jnp.logical_not(self_combine))
            def _():
                greet((seq_of(b0, b1), yl * 8 + z))
        else:
            greet((seq_of(b0, b1), yl * 8 + z))
    pl.semaphore_wait(barrier, jnp.where(self_combine, 18, 19))

    kv_out = [
        remote(src, dst, kv_send.at[n], kv_recv.at[n], partner)
        for n, (src, dst) in enumerate(kv_parts(c))
    ]
    for copy in kv_out:
        copy.start()

    def q_copy(i):
        b0, b1 = item(i)
        return remote(q_ref, qbuf.at[me_block], q_send.at[i], q_recv.at[me_block], (seq_of(b0, b1), h))

    for i in range(1, 8):
        q_copy(i).start()

    my_w = x * 2 + c

    def w_copy(d):
        return remote(w_ref, wbuf.at[my_w], w_send.at[d], w_recv.at[my_w], (seq_of(yl, (x + d) % 4), h))

    def w_forward(d):
        slot = ((x + 4 - d) % 4) * 2 + c
        return remote(wbuf.at[slot], wbuf.at[slot], wf_send.at[d], w_recv.at[slot], partner)

    for d in (1, 3, 2):
        w_copy(d).start()

    def flip(rows):
        vt[pl.ds(0, HD), rows] = vraw[rows, :].T

    vt[pl.ds(HD, VR - HD), :] = jnp.ones((VR - HD, KEYS), BF16)
    for copy in local:
        copy.wait()

    def flip_cached(core):
        def one(t, unused):
            flip(pl.ds(pl.multiple_of(core * SHARD + t * TK, TK), TK))
            return unused

        lax.fori_loop(0, SHARD // TK, one, 0)

    w_forward(0).start()
    flip_cached(c)
    for copy in kv_out:
        copy.wait_recv()
    flip_cached(1 - c)
    flip(pl.ds(CACHED, 256))

    def o_dest(i):
        b0, b1 = item(i)
        return (seq_of(yh, b1), b0 * 8 + z)

    def o_is_self(i):
        b0, b1 = item(i)
        return jnp.logical_and(self_combine, jnp.logical_and(b0 == yh, b1 == x))

    def o_copies(i):
        return (
            remote(osend.at[i], obuf.at[me_block], o_send.at[i], o_recv.at[me_block], o_dest(i)),
            remote(ssend.at[i], stbuf.at[me_block], st_send.at[i], st_recv.at[me_block], o_dest(i)),
        )

    def o_local(i):
        return (
            pltpu.make_async_copy(osend.at[i], obuf.at[me_block], o_recv.at[me_block]),
            pltpu.make_async_copy(ssend.at[i], stbuf.at[me_block], st_recv.at[me_block]),
        )

    def one_item(i, unused):
        b0, b1 = item(i)
        block = b0 * 4 + b1

        @pl.when(i > 0)
        def _():
            arrived(qbuf.at[block], q_recv.at[block])

        q = qbuf[block]
        tall = jnp.concatenate([q[:, g * HD : (g + 1) * HD] for g in range(G)], axis=0)
        wide = tall.astype(F32).T * SCALE
        high = wide.astype(BF16)
        qt[pl.ds(0, HD), :] = high
        qt[pl.ds(HD, HD), :] = (wide - high.astype(F32)).astype(BF16)

        top = jnp.full((8, COLS), -1e30, F32)
        for t in range(KEYS // TK):
            scores = jnp.dot(k2[pl.ds(t * TK, TK), :], qt[...], preferred_element_type=F32)
            if t == CACHED // TK:
                key_pos = (yl * 8 + x * 2) * 128 + lax.broadcasted_iota(jnp.int32, (TK, COLS), 0)
                row = lax.broadcasted_iota(jnp.int32, (TK, COLS), 1) % 128
                visible = key_pos <= seq_of(b0, b1) * 128 + row
                scores = jnp.where(visible, scores, -1e30)
            sbuf[pl.ds(t * TK, TK), :] = scores
            top = jnp.maximum(top, jnp.max(scores.reshape(TK // 8, 8, COLS), axis=0))
        top = jnp.max(top, axis=0, keepdims=True)
        summed = jnp.zeros((VR, COLS), F32)
        for t in range(KEYS // TK):
            weights = jnp.exp2(sbuf[pl.ds(t * TK, TK), :] - top).astype(BF16)
            summed = summed + jnp.dot(vt[:, pl.ds(t * TK, TK)], weights, preferred_element_type=F32)
        total = summed[HD : HD + 1]
        osend[i] = (summed[:HD] / total).astype(BF16)
        ssend[i] = jnp.concatenate([top, total, jnp.zeros((6, COLS), F32)], axis=0)

        is_self = o_is_self(i)

        @pl.when(is_self)
        def _():
            for copy in o_local(i):
                copy.start()

        @pl.when(jnp.logical_not(is_self))
        def _():
            for copy in o_copies(i):
                copy.start()

        return unused

    lax.fori_loop(0, 8, one_item, 0)

    for d in (1, 3, 2):
        slot = ((x + 4 - d) % 4) * 2 + c
        arrived(wbuf.at[slot], w_recv.at[slot])
        w_forward(d).start()

    for j in range(8):
        arrived(obuf.at[j], o_recv.at[j])
        arrived(stbuf.at[j], st_recv.at[j])
    tops = [stbuf[j, 0:1, :] for j in range(8)]
    top = functools.reduce(jnp.maximum, tops)
    parts = [stbuf[j, 1:2, :] * jnp.exp2(tops[j] - top) for j in range(8)]
    total = functools.reduce(jnp.add, parts)
    joined = jnp.zeros((HD, COLS), F32)
    for j in range(8):
        joined = joined + obuf[j].astype(F32) * (parts[j] / total)
    mine = yh * 8 + z
    for g in range(G):
        abuf[mine, :, pl.ds(g * HD, HD)] = joined[:, g * HD : (g + 1) * HD].T.astype(BF16)

    right = (s, yh * 8 + (z + 1) % 8)
    left = (s, yh * 8 + (z + 7) % 8)
    across = (s, (1 - yh) * 8 + z)

    def slot_of(plane, zz):
        return plane * 8 + (zz + 8) % 8

    def hand(slot, n, dev):
        return remote(abuf.at[slot], abuf.at[slot], a_send.at[n], a_recv.at[slot], dev)

    sent = []

    def send(slot, dev):
        copy = hand(slot, len(sent), dev)
        copy.start()
        sent.append(copy)

    def take(slot):
        arrived(abuf.at[slot], a_recv.at[slot])

    acc[...] = jnp.zeros_like(acc)

    def multiply(plane, zz):
        zz = (zz + 8) % 8

        for n in range(2):
            cols = pl.ds(n * 256, 256)
            acc[plane, :, cols] += jnp.dot(
                abuf[plane * 8 + zz], wbuf[zz, :, cols], preferred_element_type=F32
            )

    own, other = yh, 1 - yh
    send(mine, right)
    send(mine, left)
    send(mine, across)
    for d in range(4):
        slot = ((x + 4 - d) % 4) * 2 + 1 - c
        arrived(wbuf.at[slot], w_recv.at[slot])
    multiply(own, z)
    take(slot_of(other, z))
    send(slot_of(other, z), right)
    send(slot_of(other, z), left)
    multiply(other, z)
    for t in range(1, 5):
        take(slot_of(own, z - t))
        if t < 4:
            send(slot_of(own, z - t), right)
        if t < 4:
            take(slot_of(own, z + t))
            if t < 3:
                send(slot_of(own, z + t), left)
            take(slot_of(other, z - t))
            if t < 3:
                send(slot_of(other, z - t), right)
        take(slot_of(other, z + t))
        if t < 4:
            send(slot_of(other, z + t), left)
        multiply(own, z - t)
        if t < 4:
            multiply(own, z + t)
            multiply(other, z - t)
        multiply(other, z + t)

    csend[...] = acc[1 - yl].astype(BF16)
    swap = remote(csend, cbuf, c_send, c_recv, (seq_of(1 - yl, x), h))
    swap.start()
    swap.wait()
    out_ref[...] = (acc[yl] + cbuf[...].astype(F32)).astype(BF16)

    for copy in sent:
        copy.wait_send()
    for copy in kv_out:
        copy.wait_send()
    for i in range(1, 8):
        q_copy(i).wait_send()
    for d in (1, 2, 3):
        w_copy(d).wait_send()
    for d in range(4):
        w_forward(d).wait_send()

    def drain(i, unused):
        @pl.when(jnp.logical_not(o_is_self(i)))
        def _():
            for copy in o_copies(i):
                copy.wait_send()

        return unused

    lax.fori_loop(0, 8, drain, 0)


def local(queries, cache_keys, cache_values, new_keys, new_values, out_weight):
    dma = pltpu.SemaphoreType.DMA
    hbm = pl.BlockSpec(memory_space=pl.ANY)
    vmem = pl.BlockSpec(memory_space=pltpu.VMEM)
    return pl.pallas_call(
        kernel,
        out_shape=jax.ShapeDtypeStruct((128, 512), BF16),
        in_specs=[vmem, hbm, hbm, hbm, hbm, hbm],
        out_specs=vmem,
        scratch_shapes=[
            pltpu.VMEM((KEYS, 2 * HD), BF16),
            pltpu.VMEM((KEYS, HD), BF16),
            pltpu.VMEM((VR, KEYS), BF16),
            pltpu.VMEM((KEYS, COLS), F32),
            pltpu.VMEM((8, 128, COLS), BF16),
            pltpu.VMEM((2 * HD, COLS), BF16),
            pltpu.VMEM((8, HD, COLS), BF16),
            pltpu.VMEM((8, 8, COLS), F32),
            pltpu.VMEM((8, HD, COLS), BF16),
            pltpu.VMEM((8, 8, COLS), F32),
            pltpu.VMEM((16, 128, COLS), BF16),
            pltpu.VMEM((8, 512, 512), BF16),
            pltpu.VMEM((2, 128, 512), F32),
            pltpu.VMEM((128, 512), BF16),
            pltpu.VMEM((128, 512), BF16),
            dma((8,)), dma((6,)), dma((6,)), dma((8,)), dma((8,)),
            dma((4,)), dma((8,)), dma((4,)),
            dma((8,)), dma((8,)), dma((8,)), dma((8,)),
            dma((15,)), dma((16,)), dma, dma,
        ],
        compiler_params=pltpu.CompilerParams(
            collective_id=0, has_side_effects=True, vmem_limit_bytes=48 * 2**20
        ),
        cost_estimate=pl.CostEstimate(
            flops=11_000_000_000, bytes_accessed=4_000_000, transcendentals=18_000_000
        ),
    )(queries, cache_keys, cache_values, new_keys, new_values, out_weight)


def solution(mesh):
    placed = (
        P("seq", "head"),
        P("seq", None),
        P("seq", None),
        P("seq", None),
        P("seq", None),
        P("seq", "head"),
    )
    return jax.shard_map(
        local, mesh=mesh, in_specs=placed, out_specs=P("seq", "head"), check_vma=False
    )
```

time: 407 us -> 99.7 us (0.24)
  waiting for transfers between devices: 204 us -> 0 us
  matrix products: 131 us -> 0 us
  Pallas kernels: 0 us -> 91.6 us
  other arithmetic: 32.6 us -> 0 us
  between operations: 13.2 us -> 0.01 us
  loops' own time: 11.2 us -> 0 us
  local copies, waits for them, and re-layouts: 13.8 us -> 6.69 us
    all_gather x4 -> x0, waiting for transfers between devices: 203 us -> none  [the longest x1 86.6 us: local(): gathered = lax.all_gather(attended, 'head', axis=1, tiled=True)]
    dot_general x33 -> x0, matrix products: 131 us -> none  [the longest x16 63.5 us: attend(): jnp.einsum('kgqd,kld->kgql', query_heads, key_heads, preferred_element_ty...]
    pallas_call x0 -> x1, Pallas kernels: none -> 91.6 us  [local(): pl.pallas_call(kernel, out_shape=jax.ShapeDtypeStruct((128, 512), BF16),...]
    le x16 -> x0, other arithmetic: 16.6 us -> none  [attend(): visible = key_pos[None, :] <= query_pos[:, None]]
    dynamic_slice x20 -> x0, local copies, waits for them, and re-layouts: 13.2 us -> none  [the longest x16 10.2 us: local(): lax.scan(one_shard, initial, (key_stack, value_stack, sources))]
    reduce_sum x16 -> x0, other arithmetic: 13.1 us -> none  [attend(): weight_sum = sum_old * factor + jnp.sum(weights, axis=-1)]
    another operation x1 -> x0, loops' own time: 11.2 us -> none  [local(): lax.scan(one_shard, initial, (key_stack, value_stack, sources))]
    unnamed x6 -> x11, local copies, waits for them, and re-layouts: 0.26 us -> 6.69 us
  transfers between devices with their start and end apart: 4 -> 0, of which waited for: 3 -> 0; matrix products, arithmetic and copies ran while one was open for 42% -> 0% of each run, Pallas kernels for 0% -> 0%
where the time goes in v1:
time: 99.7 us; the launch traced here: 98.3 us
  Pallas kernels  91.6 us (92%)
  local copies, waits for them, and re-layouts  6.69 us (7%)
    pallas_call x1, Pallas kernels, local(): pl.pallas_call(kernel, out_shape=jax.ShapeDtypeStruct((128, 512), BF16),...  91.6 us
    unnamed x11, local copies, waits for them, and re-layouts  6.69 us

profile of v1, /device:TPU:6, one launch (start us, length us, event | category | flops | bytes accessed | tf_op | source)
XLA Modules:
  0.0 98.3 jit_solution(15603229541444143786)
XLA Ops:
  0.0 0.0 copy-start
  0.0 2.2 %copy-done = bf16[2048,1024]{1,0:T(8,128)(2,1)S(1)} copy-done((bf16[2048,1024]{1,0:T(8,128)(2,1)S(1)}, bf16[2048,1024]{1,0:T(8,128)(2,1)}, u32[]{:S(2)}) %copy-start) | copy-done | bytes 4194328
  2.2 0.0 copy-start.1
  2.2 1.0 %copy-done.1 = bf16[512,512]{1,0:T(8,128)(2,1)S(1)} copy-done((bf16[512,512]{1,0:T(8,128)(2,1)S(1)}, bf16[512,512]{1,0:T(8,128)(2,1)}, u32[]{:S(2)}) %copy-start.1) | copy-done | bytes 524312
  3.2 0.0 copy-start.2
  3.2 0.9 copy-done.2
  4.2 0.0 copy-start.3
  4.2 0.9 copy-done.3
  5.1 0.0 copy-start.4
  5.1 0.9 copy-done.4
  6.0 91.6 %shard_map.64 = bf16[128,512]{1,0:T(8,128)(2,1)S(1)} custom-call(bf16[128,512]{1,0:T(8,128)(2,1)S(1)} %copy-done.4, bf16[2048,1024]{1,0:T(8,128)(2,1)S(1)} %copy-done, bf16[2048,1024]{1,0:T(8,128)(2,1)} %cv_ref.1, bf16[128,1024]{1,0:T(8,128)(2,1)S(1)} %copy-done.2, bf16[128,1024]{1,0:T(8,128)(2,1)S(1)} %copy-done.3, bf16[512,512]{1,0:T(8,128)(2,1)S(1)} %copy-done.1), custom_call_target="tpu_custom_call" | custom-call | flops 11000000512 | bytes 4000000 | tf_op jit(solution)/shard_map/pallas_call | solution.py:333
  97.6 0.7 copy.8
Async XLA Ops:
  0.0 2.2 %copy-start = (bf16[2048,1024]{1,0:T(8,128)(2,1)S(1)}, bf16[2048,1024]{1,0:T(8,128)(2,1)}, u32[]{:S(2)}) copy-start(bf16[2048,1024]{1,0:T(8,128)(2,1)} %ck_ref.1) | copy-start | bytes 12582916
  2.2 1.0 %copy-start.1 = (bf16[512,512]{1,0:T(8,128)(2,1)S(1)}, bf16[512,512]{1,0:T(8,128)(2,1)}, u32[]{:S(2)}) copy-start(bf16[512,512]{1,0:T(8,128)(2,1)} %w_ref.1) | copy-start | bytes 1572868
  3.2 0.9 copy-start.2
  4.2 0.9 copy-start.3
  5.1 0.9 copy-start.4

commit v2 on v1

v2 whole, which is shorter than its diff:
```python
import functools

import jax
import jax.numpy as jnp
import numpy as np
from jax import lax
from jax.experimental import pallas as pl
from jax.experimental.pallas import tpu as pltpu
from jax.sharding import PartitionSpec as P

HD = 128
G = 4
CH = 4
RG = 128 // CH
COLS = 512
HALF = COLS // 2
SHARD = 2048
CACHED = 2 * SHARD
KEYS = CACHED + 256
TK = 256
VR = 144
SCALE = float(HD**-0.5 * np.log2(np.e))
MESH = pl.DeviceIdType.MESH
F32, BF16 = jnp.float32, jnp.bfloat16


def pieces(row):
    a = row.astype(BF16).astype(F32)
    b = (row - a).astype(BF16).astype(F32)
    return [a, b, row - a - b]


def message(result, top, total):
    zeros = jnp.zeros((10, result.shape[1]), F32)
    tail = jnp.concatenate(pieces(top) + pieces(total) + [zeros], axis=0)
    return jnp.concatenate([result.astype(BF16), tail.astype(BF16)], axis=0)


def merge(messages):
    tops, totals = [], []
    for one in messages:
        tail = one[HD:].astype(F32)
        tops.append(tail[0:1] + tail[1:2] + tail[2:3])
        totals.append(tail[3:4] + tail[4:5] + tail[5:6])
    top = functools.reduce(jnp.maximum, tops)
    parts = [b * jnp.exp2(a - top) for a, b in zip(tops, totals)]
    total = functools.reduce(jnp.add, parts)
    result = functools.reduce(
        jnp.add, [one[:HD].astype(F32) * (part / total) for one, part in zip(messages, parts)]
    )
    return result, top, total


def kernel(
    q_ref, ck_ref, cv_ref, nk_ref, nv_ref, w_ref, out_ref,
    k2, vraw, vt, sbuf, qbuf, qt, keep, ysend, yrecv, xsend, xbuf, amine, abuf, wbuf, acc, csend, cbuf,
    loc_sem, kv_send, kv_recv, q_send, q_recv, w_send, w_recv, wf_send,
    y_send, y_recv, x_send, x_recv, m_send, m_recv, z_send, z_recv, h_recv, c_send, c_recv,
):
    s = lax.axis_index("seq")
    h = lax.axis_index("head")
    yl, x, c = s // 8, (s // 2) % 4, s % 2
    yh, z = h // 8, h % 8
    me_block = yl * 4 + x
    partner = (s + 1 - 2 * c, h)

    def seq_of(a, b):
        return a * 8 + b * 2 + c

    y_mate = (seq_of(1 - yl, x), h)

    def remote(src, dst, ssem, rsem, dev):
        return pltpu.make_async_remote_copy(
            src_ref=src, dst_ref=dst, send_sem=ssem, recv_sem=rsem, device_id=dev, device_id_type=MESH
        )

    def arrived(ref, sem):
        pltpu.make_async_copy(ref, ref, sem).wait()

    def when(condition):
        return pl.when(condition)

    kv_col = pl.ds(pl.multiple_of((h // 2) * HD, HD), HD)

    def cached_rows(core):
        return pl.ds(pl.multiple_of(core * SHARD, SHARD), SHARD)

    def new_rows(core):
        return pl.ds(pl.multiple_of(CACHED + core * 128, 128), 128)

    def kv_parts(core):
        return [
            (ck_ref.at[:, kv_col], k2.at[cached_rows(core), pl.ds(0, HD)]),
            (ck_ref.at[:, kv_col], k2.at[cached_rows(core), pl.ds(HD, HD)]),
            (nk_ref.at[:, kv_col], k2.at[new_rows(core), pl.ds(0, HD)]),
            (nk_ref.at[:, kv_col], k2.at[new_rows(core), pl.ds(HD, HD)]),
            (cv_ref.at[:, kv_col], vraw.at[cached_rows(core), :]),
            (nv_ref.at[:, kv_col], vraw.at[new_rows(core), :]),
        ]

    local = [
        pltpu.make_async_copy(src, dst, loc_sem.at[n]) for n, (src, dst) in enumerate(kv_parts(c))
    ]
    local.append(pltpu.make_async_copy(w_ref, wbuf.at[x * 2 + c], loc_sem.at[6]))
    local.append(pltpu.make_async_copy(q_ref, qbuf.at[me_block], loc_sem.at[7]))
    for copy in local:
        copy.start()

    barrier = pltpu.get_barrier_semaphore()

    def greet(dev):
        pl.semaphore_signal(barrier, inc=1, device_id=dev, device_id_type=MESH)

    def peer(n):
        return (seq_of((yl + n % 2) % 2, (x + n // 2) % 4), h)

    for n in range(1, 8):
        greet(peer(n))
    right = (s, yh * 8 + (z + 1) % 8)
    left = (s, yh * 8 + (z + 7) % 8)
    greet(partner)
    greet(right)
    greet(left)
    for a in range(2):
        @when(jnp.logical_or(yl != yh, yl != a))
        def _():
            greet((seq_of(a, x), yl * 8 + z))

    pl.semaphore_wait(barrier, jnp.where(yl == yh, 11, 12))

    kv_out = [
        remote(src, dst, kv_send.at[n], kv_recv.at[n], partner)
        for n, (src, dst) in enumerate(kv_parts(c))
    ]

    def q_copy(g, n):
        rows = pl.ds(pl.multiple_of(g * RG, RG), RG)
        return remote(
            q_ref.at[rows], qbuf.at[me_block, rows], q_send.at[g, n], q_recv.at[g, me_block], peer(n)
        )

    def q_start(g):
        for n in (1, 2, 6, 3, 7, 4, 5):
            q_copy(g, n).start()

    q_start(0)
    for copy in kv_out:
        copy.start()

    my_w = x * 2 + c

    def w_copy(d):
        return remote(w_ref, wbuf.at[my_w], w_send.at[d], w_recv.at[my_w], (seq_of(yl, (x + d) % 4), h))

    def w_slot(d):
        return ((x + 4 - d) % 4) * 2 + c

    def w_forward(d):
        slot = w_slot(d)
        return remote(wbuf.at[slot], wbuf.at[slot], wf_send.at[d], w_recv.at[slot], partner)

    def w_hand_on(d):
        arrived(wbuf.at[w_slot(d)], w_recv.at[w_slot(d)])
        w_forward(d).start()

    def flip(rows):
        vt[pl.ds(0, HD), rows] = vraw[rows, :].T

    def flip_cached(core):
        def one(t, unused):
            flip(pl.ds(pl.multiple_of(core * SHARD + t * TK, TK), TK))
            return unused

        lax.fori_loop(0, SHARD // TK, one, 0)

    vt[pl.ds(HD, VR - HD), :] = jnp.ones((VR - HD, KEYS), BF16)
    for copy in local:
        copy.wait()
    flip_cached(c)

    def reduce_y_start(i):
        return remote(ysend.at[i], yrecv.at[i], y_send.at[i], y_recv.at[i], y_mate)

    def x_dest(i, k):
        return (x + 2 * (i % 2) + k) % 4

    def x_copy(i, k):
        return remote(
            xsend.at[i, k], xbuf.at[i // 2, x], x_send.at[i, k], x_recv.at[i // 2, x],
            (seq_of(yl, x_dest(i, k)), h),
        )

    def stage_x(i):
        arrived(yrecv.at[i], y_recv.at[i])
        merged = message(*merge([keep[i % 2], yrecv[i]]))
        for k in range(2):
            xsend[i, k] = merged[:, k * HD : (k + 1) * HD]
        x_copy(i, 1).start()

        @when(i % 2 == 0)
        def _():
            pltpu.make_async_copy(xsend.at[i, 0], xbuf.at[i // 2, x], x_recv.at[i // 2, x]).start()

        @when(i % 2 == 1)
        def _():
            x_copy(i, 0).start()

    def m_copy(g, a):
        return remote(
            amine.at[g], abuf.at[z, g, yl], m_send.at[g, a], m_recv.at[g, yl], (seq_of(yh, x), a * 8 + z)
        )

    def m_is_self(a):
        return jnp.logical_and(yl == yh, yh == a)

    def stage_m(g):
        for j in range(4):
            arrived(xbuf.at[g, j], x_recv.at[g, j])
        result, _, _ = merge([xbuf[g, j] for j in range(4)])
        turned = result.T.astype(BF16)
        for n in range(G):
            amine[g, :, pl.ds(n * HD, HD)] = turned[n * RG : (n + 1) * RG]
        for a in range(2):
            @when(m_is_self(a))
            def _():
                pltpu.make_async_copy(amine.at[g], abuf.at[z, g, yl], m_recv.at[g, yl]).start()

            @when(jnp.logical_not(m_is_self(a)))
            def _():
                m_copy(g, a).start()

    def zz(d):
        return (z + 8 + d) % 8

    def z_copy(g, t, way):
        slot = zz(-t) if way == 0 else zz(t)
        dev = right if way == 0 else left
        if t < 3:
            ref, sem = abuf.at[slot, g], z_recv.at[g, slot]
        else:
            ref, sem = abuf.at[slot, g, way], h_recv.at[g, way]
        return remote(ref, ref, z_send.at[g, t, way], sem, dev)

    def z_wait(g, t):
        if t == 0:
            for a in range(2):
                arrived(abuf.at[z, g, a], m_recv.at[g, a])
        elif t < 4:
            for d in (-t, t):
                arrived(abuf.at[zz(d), g], z_recv.at[g, zz(d)])
        else:
            for a in range(2):
                arrived(abuf.at[zz(4), g, a], h_recv.at[g, a])

    def stage_z(g, t):
        z_wait(g, t)
        if t < 4:
            for way in range(2):
                z_copy(g, t, way).start()

    def one_item(i, unused):
        g, sub = i // 2, i % 2
        places = [((yl + dy) % 2, (x + 2 * sub + k) % 4) for dy in range(2) for k in range(2)]

        @when(jnp.logical_and(sub == 0, g < CH - 1))
        def _():
            q_start(g + 1)

        rows = pl.ds(pl.multiple_of(g * RG, RG), RG)
        for n, (a, b) in enumerate(places):
            block = a * 4 + b
            if n == 0:
                @when(sub > 0)
                def _():
                    arrived(qbuf.at[block, rows], q_recv.at[g, block])
            else:
                arrived(qbuf.at[block, rows], q_recv.at[g, block])
        tall = jnp.concatenate(
            [qbuf[a * 4 + b, rows, pl.ds(n * HD, HD)] for a, b in places for n in range(G)], axis=0
        )
        wide = tall.astype(F32).T * SCALE
        high = wide.astype(BF16)
        qt[pl.ds(0, HD), :] = high
        qt[pl.ds(HD, HD), :] = (wide - high.astype(F32)).astype(BF16)

        def score(rows):
            return jnp.dot(k2[rows, :], qt[...], preferred_element_type=F32)

        def highest(top, scores):
            return jnp.maximum(top, jnp.max(scores.reshape(TK // 8, 8, COLS), axis=0))

        top = jnp.full((8, COLS), -1e30, F32)
        for core in (c, 1 - c):
            for t in range(SHARD // TK):
                rows = pl.ds(pl.multiple_of(core * SHARD + t * TK, TK), TK)
                scores = score(rows)
                sbuf[rows, :] = scores
                top = highest(top, scores)
            if core is c:
                @when(i == 0)
                def _():
                    for copy in kv_out[:4]:
                        copy.wait_recv()

        col = lax.broadcasted_iota(jnp.int32, (1, COLS), 1)
        base = jnp.zeros((1, COLS), jnp.int32)
        for n, (a, b) in enumerate(places):
            base = jnp.where(col // HD == n, seq_of(a, b) * 128, base)
        query_pos = base + g * RG + col % RG
        rows = pl.ds(CACHED, TK)
        key_pos = (yl * 8 + x * 2) * 128 + lax.broadcasted_iota(jnp.int32, (TK, COLS), 0)
        scores = jnp.where(key_pos <= query_pos, score(rows), -1e30)
        sbuf[rows, :] = scores
        top = jnp.max(highest(top, scores), axis=0, keepdims=True)

        @when(i == 0)
        def _():
            for copy in kv_out[4:]:
                copy.wait_recv()
            flip_cached(1 - c)
            flip(pl.ds(CACHED, 256))

        @when(i > 0)
        def _():
            stage_x(i - 1)

        @when(jnp.logical_and(sub == 1, i >= 3))
        def _():
            stage_z((i - 3) // 2, 0)

        @when(jnp.logical_and(sub == 0, i >= 4))
        def _():
            stage_z((i - 4) // 2, 2)

        summed = jnp.zeros((VR, COLS), F32)
        for t in range(KEYS // TK):
            weights = jnp.exp2(sbuf[pl.ds(t * TK, TK), :] - top).astype(BF16)
            summed = summed + jnp.dot(vt[:, pl.ds(t * TK, TK)], weights, preferred_element_type=F32)
        total = summed[HD : HD + 1]
        packed = message(summed[:HD] / total, top, total)
        keep[i % 2] = packed[:, :HALF]
        ysend[i] = packed[:, HALF:]
        reduce_y_start(i).start()

        @when(jnp.logical_and(sub == 0, i >= 2))
        def _():
            stage_m((i - 2) // 2)

        @when(jnp.logical_and(sub == 1, i >= 3))
        def _():
            stage_z((i - 3) // 2, 1)

        @when(jnp.logical_and(sub == 0, i >= 4))
        def _():
            stage_z((i - 4) // 2, 3)

        @when(i == 0)
        def _():
            w_forward(0).start()
            w_copy(1).start()

        @when(i == 1)
        def _():
            w_copy(3).start()

        @when(i == 2)
        def _():
            w_copy(2).start()

        @when(i == 5)
        def _():
            w_hand_on(1)

        @when(i == 6)
        def _():
            w_hand_on(3)

        return unused

    lax.fori_loop(0, 2 * CH, one_item, 0)

    stage_x(2 * CH - 1)
    stage_z(CH - 2, 2)
    w_hand_on(2)
    stage_m(CH - 1)
    stage_z(CH - 2, 3)
    for d in range(4):
        slot = ((x + 4 - d) % 4) * 2 + 1 - c
        arrived(wbuf.at[slot], w_recv.at[slot])
    stage_z(CH - 1, 0)

    def multiply(first, count, place):
        rows = 2 * RG * count
        block = abuf[place, first : first + count].reshape(rows, COLS)
        return jnp.dot(block, wbuf[place], preferred_element_type=F32).reshape(count, 2, RG, 512)

    for g in range(CH - 1):
        z_wait(g, 4)

    acc[...] = jnp.zeros_like(acc)

    def early(place, unused):
        acc[0 : CH - 1] += multiply(0, CH - 1, place)
        return unused

    lax.fori_loop(0, 4, early, 0)
    stage_z(CH - 1, 1)
    lax.fori_loop(4, 8, early, 0)
    stage_z(CH - 1, 2)
    for g in range(CH - 1):
        csend[g] = acc[g, 1 - yl].astype(BF16)

    def swap(n):
        some = pl.ds(0, CH - 1) if n == 0 else pl.ds(CH - 1, 1)
        return remote(csend.at[some], cbuf.at[some], c_send.at[n], c_recv.at[n], y_mate)

    swap(0).start()

    def late(d):
        acc[CH - 1 :] += multiply(CH - 1, 1, zz(d))

    late(0)
    late(-1)
    late(1)
    stage_z(CH - 1, 3)
    late(-2)
    late(2)
    late(-3)
    late(3)
    z_wait(CH - 1, 4)
    late(4)
    csend[CH - 1] = acc[CH - 1, 1 - yl].astype(BF16)
    swap(1).start()
    swap(0).wait_recv()
    for g in range(CH):
        if g == CH - 1:
            swap(1).wait_recv()
        out_ref[pl.ds(g * RG, RG), :] = (acc[g, yl] + cbuf[g].astype(F32)).astype(BF16)

    for n in range(2):
        swap(n).wait_send()
    for copy in kv_out:
        copy.wait_send()
    for d in range(4):
        w_forward(d).wait_send()
        if d > 0:
            w_copy(d).wait_send()

    def drain_chunk(g, unused):
        for n in range(1, 8):
            q_copy(g, n).wait_send()
        for a in range(2):
            @when(jnp.logical_not(m_is_self(a)))
            def _():
                m_copy(g, a).wait_send()

        for t in range(4):
            for way in range(2):
                z_copy(g, t, way).wait_send()
        return unused

    lax.fori_loop(0, CH, drain_chunk, 0)

    def drain_item(i, unused):
        reduce_y_start(i).wait_send()
        x_copy(i, 1).wait_send()

        @when(i % 2 == 1)
        def _():
            x_copy(i, 0).wait_send()

        return unused

    lax.fori_loop(0, 2 * CH, drain_item, 0)


def local(queries, cache_keys, cache_values, new_keys, new_values, out_weight):
    dma = pltpu.SemaphoreType.DMA
    hbm = pl.BlockSpec(memory_space=pltpu.HBM)
    vmem = pl.BlockSpec(memory_space=pltpu.VMEM)
    items = 2 * CH
    return pl.pallas_call(
        kernel,
        out_shape=jax.ShapeDtypeStruct((128, 512), BF16),
        in_specs=[vmem, hbm, hbm, hbm, hbm, hbm],
        out_specs=vmem,
        scratch_shapes=[
            pltpu.VMEM((KEYS, 2 * HD), BF16),
            pltpu.VMEM((KEYS, HD), BF16),
            pltpu.VMEM((VR, KEYS), BF16),
            pltpu.VMEM((KEYS, COLS), F32),
            pltpu.VMEM((8, 128, 512), BF16),
            pltpu.VMEM((2 * HD, COLS), BF16),
            pltpu.VMEM((2, VR, HALF), BF16),
            pltpu.VMEM((items, VR, HALF), BF16),
            pltpu.VMEM((items, VR, HALF), BF16),
            pltpu.VMEM((items, 2, VR, HD), BF16),
            pltpu.VMEM((CH, 4, VR, HD), BF16),
            pltpu.VMEM((CH, RG, 512), BF16),
            pltpu.VMEM((8, CH, 2, RG, 512), BF16),
            pltpu.VMEM((8, 512, 512), BF16),
            pltpu.VMEM((CH, 2, RG, 512), F32),
            pltpu.VMEM((CH, RG, 512), BF16),
            pltpu.VMEM((CH, RG, 512), BF16),
            dma((8,)), dma((6,)), dma((6,)), dma((CH, 8)), dma((CH, 8)),
            dma((4,)), dma((8,)), dma((4,)),
            dma((items,)), dma((items,)), dma((items, 2)), dma((CH, 4)),
            dma((CH, 2)), dma((CH, 2)), dma((CH, 4, 2)), dma((CH, 8)), dma((CH, 2)),
            dma((2,)), dma((2,)),
        ],
        compiler_params=pltpu.CompilerParams(
            collective_id=0, has_side_effects=True, vmem_limit_bytes=48 * 2**20
        ),
        cost_estimate=pl.CostEstimate(
            flops=11_000_000_000, bytes_accessed=4_000_000, transcendentals=18_000_000
        ),
    )(queries, cache_keys, cache_values, new_keys, new_values, out_weight)


def solution(mesh):
    placed = (
        P("seq", "head"),
        P("seq", None),
        P("seq", None),
        P("seq", None),
        P("seq", None),
        P("seq", "head"),
    )
    return jax.shard_map(
        local, mesh=mesh, in_specs=placed, out_specs=P("seq", "head"), check_vma=False
    )
```

time: 99.7 us -> 113 us (1.13)
  Pallas kernels: 91.6 us -> 104 us
    pallas_call x1, Pallas kernels: 91.6 us -> 104 us  [local(): pl.pallas_call(kernel, out_shape=jax.ShapeDtypeStruct((128, 512), BF16),...]
where the time goes in v2:
time: 113 us; the launch traced here: 111 us
  Pallas kernels  104 us (92%)
  local copies, waits for them, and re-layouts  6.69 us (6%)
    pallas_call x1, Pallas kernels, local(): pl.pallas_call(kernel, out_shape=jax.ShapeDtypeStruct((128, 512), BF16),...  104 us
    unnamed x11, local copies, waits for them, and re-layouts  6.69 us

profile of v2, /device:TPU:6, one launch (start us, length us, event | category | flops | bytes accessed | tf_op | source)
XLA Modules:
  0.0 110.9 jit_solution(14299137692623667983)
XLA Ops:
  0.0 0.0 copy-start
  0.0 2.2 %copy-done = bf16[2048,1024]{1,0:T(8,128)(2,1)S(1)} copy-done((bf16[2048,1024]{1,0:T(8,128)(2,1)S(1)}, bf16[2048,1024]{1,0:T(8,128)(2,1)}, u32[]{:S(2)}) %copy-start) | copy-done | bytes 4194328
  2.2 0.0 copy-start.1
  2.2 1.0 copy-done.1
  3.2 0.0 copy-start.2
  3.2 0.9 copy-done.2
  4.2 0.0 copy-start.3
  4.2 0.9 copy-done.3
  5.1 0.0 copy-start.4
  5.1 0.9 copy-done.4
  6.0 104.2 %shard_map.64 = bf16[128,512]{1,0:T(8,128)(2,1)S(1)} custom-call(bf16[128,512]{1,0:T(8,128)(2,1)S(1)} %copy-done.4, bf16[2048,1024]{1,0:T(8,128)(2,1)S(1)} %copy-done, bf16[2048,1024]{1,0:T(8,128)(2,1)} %cv_ref.1, bf16[128,1024]{1,0:T(8,128)(2,1)S(1)} %copy-done.2, bf16[128,1024]{1,0:T(8,128)(2,1)S(1)} %copy-done.3, bf16[512,512]{1,0:T(8,128)(2,1)S(1)} %copy-done.1), custom_call_target="tpu_custom_call" | custom-call | flops 11000000512 | bytes 4000000 | tf_op jit(solution)/shard_map/pallas_call | solution.py:482
  110.2 0.7 copy.8
Async XLA Ops:
  0.0 2.2 %copy-start = (bf16[2048,1024]{1,0:T(8,128)(2,1)S(1)}, bf16[2048,1024]{1,0:T(8,128)(2,1)}, u32[]{:S(2)}) copy-start(bf16[2048,1024]{1,0:T(8,128)(2,1)} %ck_ref.1) | copy-start | bytes 12582916
  2.2 1.0 copy-start.1
  3.2 0.9 copy-start.2
  4.2 0.9 copy-start.3
  5.1 0.9 copy-start.4

commit v3 on v2

v3 whole, which is shorter than its diff:
```python
import functools

import jax
import jax.numpy as jnp
import numpy as np
from jax import lax
from jax.experimental import pallas as pl
from jax.experimental.pallas import tpu as pltpu
from jax.sharding import PartitionSpec as P

HD = 128
G = 4
CH = 4
RG = 128 // CH
COLS = 512
SHARD = 2048
CACHED = 2 * SHARD
KEYS = CACHED + 256
TK = 256
VR = 144
SCALE = float(HD**-0.5 * np.log2(np.e))
MESH = pl.DeviceIdType.MESH
F32, BF16 = jnp.float32, jnp.bfloat16


def pieces(row):
    a = row.astype(BF16).astype(F32)
    b = (row - a).astype(BF16).astype(F32)
    return [a, b, row - a - b]


def message(result, top, total):
    zeros = jnp.zeros((10, result.shape[1]), F32)
    tail = jnp.concatenate(pieces(top) + pieces(total) + [zeros], axis=0)
    return jnp.concatenate([result.astype(BF16), tail.astype(BF16)], axis=0)


def merge(messages):
    tops, totals = [], []
    for one in messages:
        tail = one[HD:].astype(F32)
        tops.append(tail[0:1] + tail[1:2] + tail[2:3])
        totals.append(tail[3:4] + tail[4:5] + tail[5:6])
    top = functools.reduce(jnp.maximum, tops)
    parts = [b * jnp.exp2(a - top) for a, b in zip(tops, totals)]
    total = functools.reduce(jnp.add, parts)
    result = functools.reduce(
        jnp.add, [one[:HD].astype(F32) * (part / total) for one, part in zip(messages, parts)]
    )
    return result


def kernel(
    q_ref, ck_ref, cv_ref, nk_ref, nv_ref, w_ref, out_ref,
    k2, vraw, vt, sbuf, qbuf, qt, osend, obuf, amine, abuf, wbuf, acc, csend, cbuf,
    loc_sem, kv_send, kv_recv, q_send, q_recv, w_send, w_recv, wf_send,
    o_send, o_recv, m_send, m_recv, z_send, z_recv, h_recv, c_send, c_recv,
):
    s = lax.axis_index("seq")
    h = lax.axis_index("head")
    yl, x, c = s // 8, (s // 2) % 4, s % 2
    yh, z = h // 8, h % 8
    me_block = yl * 4 + x
    partner = (s + 1 - 2 * c, h)

    def seq_of(a, b):
        return a * 8 + b * 2 + c

    y_mate = (seq_of(1 - yl, x), h)

    def remote(src, dst, ssem, rsem, dev):
        return pltpu.make_async_remote_copy(
            src_ref=src, dst_ref=dst, send_sem=ssem, recv_sem=rsem, device_id=dev, device_id_type=MESH
        )

    def arrived(ref, sem):
        pltpu.make_async_copy(ref, ref, sem).wait()

    kv_col = pl.ds(pl.multiple_of((h // 2) * HD, HD), HD)

    def cached_rows(core):
        return pl.ds(pl.multiple_of(core * SHARD, SHARD), SHARD)

    def new_rows(core):
        return pl.ds(pl.multiple_of(CACHED + core * 128, 128), 128)

    def kv_parts(core):
        return [
            (ck_ref.at[:, kv_col], k2.at[cached_rows(core), pl.ds(0, HD)]),
            (ck_ref.at[:, kv_col], k2.at[cached_rows(core), pl.ds(HD, HD)]),
            (nk_ref.at[:, kv_col], k2.at[new_rows(core), pl.ds(0, HD)]),
            (nk_ref.at[:, kv_col], k2.at[new_rows(core), pl.ds(HD, HD)]),
            (cv_ref.at[:, kv_col], vraw.at[cached_rows(core), :]),
            (nv_ref.at[:, kv_col], vraw.at[new_rows(core), :]),
        ]

    local = [
        pltpu.make_async_copy(src, dst, loc_sem.at[n]) for n, (src, dst) in enumerate(kv_parts(c))
    ]
    local.append(pltpu.make_async_copy(w_ref, wbuf.at[x * 2 + c], loc_sem.at[6]))
    local.append(pltpu.make_async_copy(q_ref, qbuf.at[me_block], loc_sem.at[7]))
    for copy in local:
        copy.start()

    barrier = pltpu.get_barrier_semaphore()

    def greet(dev):
        pl.semaphore_signal(barrier, inc=1, device_id=dev, device_id_type=MESH)

    def peer(n):
        return (seq_of((yl + n % 2) % 2, (x + n // 2) % 4), h)

    for n in range(1, 8):
        greet(peer(n))
    greet(partner)
    for d in (1, 2, 6, 7):
        greet((s, yh * 8 + (z + d) % 8))
        for a in range(2):
            greet((seq_of(a, x), yl * 8 + (z + d) % 8))
    for a in range(2):
        @pl.when(jnp.logical_or(yl != yh, yl != a))
        def _():
            greet((seq_of(a, x), yl * 8 + z))

    pl.semaphore_wait(barrier, jnp.where(yl == yh, 21, 22))

    kv_out = [
        remote(src, dst, kv_send.at[n], kv_recv.at[n], partner)
        for n, (src, dst) in enumerate(kv_parts(c))
    ]

    def q_copy(g, n):
        rows = pl.ds(pl.multiple_of(g * RG, RG), RG)
        return remote(
            q_ref.at[rows], qbuf.at[me_block, rows], q_send.at[g, n], q_recv.at[g, me_block], peer(n)
        )

    def q_start(g):
        for n in (1, 2, 6, 3, 7, 4, 5):
            q_copy(g, n).start()

    q_start(0)
    for copy in kv_out:
        copy.start()

    my_w = x * 2 + c

    def w_rows(j):
        return pl.ds(pl.multiple_of(j * 128, 128), 128)

    def w_copy(d, j):
        return remote(
            w_ref.at[w_rows(j)], wbuf.at[my_w, w_rows(j)], w_send.at[d, j], w_recv.at[my_w, j],
            (seq_of(yl, (x + d) % 4), h),
        )

    def w_start(j):
        for d in (1, 3, 2):
            w_copy(d, j).start()

    def w_forward(d):
        return remote(w_ref, wbuf.at[my_w], wf_send.at[0, 0], w_recv.at[my_w, 0], partner)

    def w_pass(d, j):
        slot = ((x + 4 - d) % 4) * 2 + c
        ref = wbuf.at[slot, w_rows(j)]
        return remote(ref, ref, wf_send.at[d, j], w_recv.at[slot, j], partner)

    def w_hand_on(j):
        for d in (1, 3, 2):
            slot = ((x + 4 - d) % 4) * 2 + c
            arrived(wbuf.at[slot, w_rows(j)], w_recv.at[slot, j])
            w_pass(d, j).start()

    def flip(rows):
        vt[pl.ds(0, HD), rows] = vraw[rows, :].T

    def flip_cached(core):
        def one(t, unused):
            flip(pl.ds(pl.multiple_of(core * SHARD + t * TK, TK), TK))
            return unused

        lax.fori_loop(0, SHARD // TK, one, 0)

    vt[pl.ds(HD, VR - HD), :] = jnp.ones((VR - HD, KEYS), BF16)
    for copy in local:
        copy.wait()
    flip_cached(c)

    def o_place(i, n):
        return (yl + n // 2) % 2, (x + 2 * (i % 2) + n % 2) % 4

    def o_copy(i, n):
        p, q = o_place(i, n)
        return remote(
            osend.at[i, n], obuf.at[i // 2, me_block], o_send.at[i, n], o_recv.at[i // 2, me_block],
            (seq_of(p, q), h),
        )

    def stage_o(i):
        for n in (2, 1, 3):
            o_copy(i, n).start()

        @pl.when(i % 2 == 0)
        def _():
            pltpu.make_async_copy(
                osend.at[i, 0], obuf.at[i // 2, me_block], o_recv.at[i // 2, me_block]
            ).start()

        @pl.when(i % 2 == 1)
        def _():
            o_copy(i, 0).start()

    def zz(d):
        return (z + 8 + d) % 8

    def m_copy(g, a, d):
        return remote(
            amine.at[g], abuf.at[z, g, yl], m_send.at[g, a, d + 2], m_recv.at[g, z, yl],
            (seq_of(yh, x), a * 8 + zz(d)),
        )

    def m_is_self(a):
        return jnp.logical_and(yl == yh, yh == a)

    def stage_m(g):
        for j in range(8):
            arrived(obuf.at[g, j], o_recv.at[g, j])
        result = merge([obuf[g, j] for j in range(8)])
        turned = result.T.astype(BF16)
        for n in range(G):
            amine[g, :, pl.ds(n * HD, HD)] = turned[n * RG : (n + 1) * RG]
        for d in (-2, 2, -1, 1):
            for a in range(2):
                m_copy(g, a, d).start()
        for a in range(2):
            @pl.when(m_is_self(a))
            def _():
                pltpu.make_async_copy(amine.at[g], abuf.at[z, g, yl], m_recv.at[g, z, yl]).start()

            @pl.when(jnp.logical_not(m_is_self(a)))
            def _():
                m_copy(g, a, 0).start()

    def m_wait(g, d):
        for a in range(2):
            arrived(abuf.at[zz(d), g, a], m_recv.at[g, zz(d), a])

    def z_copies(g):
        near, far = abuf.at[zz(-2), g], abuf.at[zz(2), g]
        half, other = abuf.at[zz(-2), g, 0], abuf.at[zz(2), g, 1]
        return (
            remote(half, half, z_send.at[g, 0], h_recv.at[g, 0], (s, yh * 8 + zz(2))),
            remote(other, other, z_send.at[g, 1], h_recv.at[g, 1], (s, yh * 8 + zz(-2))),
            remote(near, near, z_send.at[g, 2], z_recv.at[g, 0], (s, yh * 8 + zz(1))),
            remote(far, far, z_send.at[g, 3], z_recv.at[g, 1], (s, yh * 8 + zz(-1))),
        )

    def stage_z(g):
        m_wait(g, -2)
        m_wait(g, 2)
        for copy in z_copies(g):
            copy.start()

    def z_wait(g):
        for d in (-1, 0, 1):
            m_wait(g, d)
        arrived(abuf.at[zz(-3), g], z_recv.at[g, 0])
        arrived(abuf.at[zz(3), g], z_recv.at[g, 1])
        for a in range(2):
            arrived(abuf.at[zz(4), g, a], h_recv.at[g, a])

    def one_item(i, unused):
        g, sub = i // 2, i % 2
        places = [((yl + dy) % 2, (x + 2 * sub + k) % 4) for dy in range(2) for k in range(2)]

        @pl.when(jnp.logical_and(sub == 0, g < CH - 1))
        def _():
            q_start(g + 1)

        rows = pl.ds(pl.multiple_of(g * RG, RG), RG)
        for n, (a, b) in enumerate(places):
            block = a * 4 + b
            if n == 0:
                @pl.when(sub > 0)
                def _():
                    arrived(qbuf.at[block, rows], q_recv.at[g, block])
            else:
                arrived(qbuf.at[block, rows], q_recv.at[g, block])
        tall = jnp.concatenate(
            [qbuf[a * 4 + b, rows, pl.ds(n * HD, HD)] for a, b in places for n in range(G)], axis=0
        )
        wide = tall.astype(F32).T * SCALE
        high = wide.astype(BF16)
        qt[pl.ds(0, HD), :] = high
        qt[pl.ds(HD, HD), :] = (wide - high.astype(F32)).astype(BF16)

        def score(rows):
            return jnp.dot(k2[rows, :], qt[...], preferred_element_type=F32)

        def highest(top, scores):
            return jnp.maximum(top, jnp.max(scores.reshape(TK // 8, 8, COLS), axis=0))

        top = jnp.full((8, COLS), -1e30, F32)
        for core in (c, 1 - c):
            for t in range(SHARD // TK):
                rows = pl.ds(pl.multiple_of(core * SHARD + t * TK, TK), TK)
                scores = score(rows)
                sbuf[rows, :] = scores
                top = highest(top, scores)
            if core is c:
                @pl.when(i == 0)
                def _():
                    for copy in kv_out[:4]:
                        copy.wait_recv()

        col = lax.broadcasted_iota(jnp.int32, (1, COLS), 1)
        base = jnp.zeros((1, COLS), jnp.int32)
        for n, (a, b) in enumerate(places):
            base = jnp.where(col // HD == n, seq_of(a, b) * 128, base)
        query_pos = base + g * RG + col % RG
        rows = pl.ds(CACHED, TK)
        key_pos = (yl * 8 + x * 2) * 128 + lax.broadcasted_iota(jnp.int32, (TK, COLS), 0)
        scores = jnp.where(key_pos <= query_pos, score(rows), -1e30)
        sbuf[rows, :] = scores
        top = jnp.max(highest(top, scores), axis=0, keepdims=True)

        @pl.when(i == 0)
        def _():
            for copy in kv_out[4:]:
                copy.wait_recv()
            flip_cached(1 - c)
            flip(pl.ds(CACHED, 256))

        @pl.when(jnp.logical_and(sub == 1, i >= 3))
        def _():
            stage_m((i - 3) // 2)

        summed = jnp.zeros((VR, COLS), F32)
        for t in range(KEYS // TK):
            weights = jnp.exp2(sbuf[pl.ds(t * TK, TK), :] - top).astype(BF16)
            summed = summed + jnp.dot(vt[:, pl.ds(t * TK, TK)], weights, preferred_element_type=F32)
        total = summed[HD : HD + 1]
        packed = message(summed[:HD] / total, top, total)
        for n in range(4):
            osend[i, n] = packed[:, n * HD : (n + 1) * HD]
        stage_o(i)

        @pl.when(jnp.logical_and(sub == 0, i >= 4))
        def _():
            stage_z((i - 4) // 2)

        @pl.when(i == 0)
        def _():
            w_forward(0).start()

        @pl.when(jnp.logical_and(sub == 1, i < 6))
        def _():
            w_start(i // 2)

        @pl.when(jnp.logical_and(sub == 0, i >= 4))
        def _():
            w_hand_on((i - 4) // 2)

        return unused

    lax.fori_loop(0, 2 * CH, one_item, 0)

    stage_m(CH - 1)
    w_start(3)
    stage_z(CH - 2)
    w_hand_on(2)
    stage_z(CH - 1)
    w_hand_on(3)
    for g in range(CH - 1):
        z_wait(g)
    slot = my_w + 1 - 2 * c
    arrived(wbuf.at[slot], w_recv.at[slot, 0])
    for j in range(4):
        for d in (1, 3, 2):
            slot = ((x + 4 - d) % 4) * 2 + 1 - c
            arrived(wbuf.at[slot, w_rows(j)], w_recv.at[slot, j])

    def multiply(first, count, place):
        rows = 2 * RG * count
        block = abuf[place, first : first + count].reshape(rows, COLS)
        return jnp.dot(block, wbuf[place], preferred_element_type=F32).reshape(count, 2, RG, 512)

    acc[...] = jnp.zeros_like(acc)

    def early(place, unused):
        acc[0 : CH - 1] += multiply(0, CH - 1, place)
        return unused

    lax.fori_loop(0, 8, early, 0)
    for g in range(CH - 1):
        csend[g] = acc[g, 1 - yl].astype(BF16)

    def swap(n):
        some = pl.ds(0, CH - 1) if n == 0 else pl.ds(CH - 1, 1)
        return remote(csend.at[some], cbuf.at[some], c_send.at[n], c_recv.at[n], y_mate)

    swap(0).start()

    def late(d):
        acc[CH - 1 :] += multiply(CH - 1, 1, zz(d))

    z_wait(CH - 1)
    for d in range(8):
        late(d - 4)
    csend[CH - 1] = acc[CH - 1, 1 - yl].astype(BF16)
    swap(1).start()
    swap(0).wait_recv()
    for g in range(CH):
        if g == CH - 1:
            swap(1).wait_recv()
        out_ref[pl.ds(g * RG, RG), :] = (acc[g, yl] + cbuf[g].astype(F32)).astype(BF16)

    for n in range(2):
        swap(n).wait_send()
    for copy in kv_out:
        copy.wait_send()
    w_forward(0).wait_send()
    for d in range(1, 4):
        for j in range(4):
            w_copy(d, j).wait_send()
            w_pass(d, j).wait_send()

    def drain_chunk(g, unused):
        for n in range(1, 8):
            q_copy(g, n).wait_send()
        for a in range(2):
            for d in (-2, -1, 1, 2):
                m_copy(g, a, d).wait_send()

            @pl.when(jnp.logical_not(m_is_self(a)))
            def _():
                m_copy(g, a, 0).wait_send()

        for copy in z_copies(g):
            copy.wait_send()
        return unused

    lax.fori_loop(0, CH, drain_chunk, 0)

    def drain_item(i, unused):
        for n in range(1, 4):
            o_copy(i, n).wait_send()

        @pl.when(i % 2 == 1)
        def _():
            o_copy(i, 0).wait_send()

        return unused

    lax.fori_loop(0, 2 * CH, drain_item, 0)


def local(queries, cache_keys, cache_values, new_keys, new_values, out_weight):
    dma = pltpu.SemaphoreType.DMA
    hbm = pl.BlockSpec(memory_space=pltpu.HBM)
    vmem = pl.BlockSpec(memory_space=pltpu.VMEM)
    items = 2 * CH
    return pl.pallas_call(
        kernel,
        out_shape=jax.ShapeDtypeStruct((128, 512), BF16),
        in_specs=[vmem, hbm, hbm, hbm, hbm, hbm],
        out_specs=vmem,
        scratch_shapes=[
            pltpu.VMEM((KEYS, 2 * HD), BF16),
            pltpu.VMEM((KEYS, HD), BF16),
            pltpu.VMEM((VR, KEYS), BF16),
            pltpu.VMEM((KEYS, COLS), F32),
            pltpu.VMEM((8, 128, 512), BF16),
            pltpu.VMEM((2 * HD, COLS), BF16),
            pltpu.VMEM((items, 4, VR, HD), BF16),
            pltpu.VMEM((CH, 8, VR, HD), BF16),
            pltpu.VMEM((CH, RG, 512), BF16),
            pltpu.VMEM((8, CH, 2, RG, 512), BF16),
            pltpu.VMEM((8, 512, 512), BF16),
            pltpu.VMEM((CH, 2, RG, 512), F32),
            pltpu.VMEM((CH, RG, 512), BF16),
            pltpu.VMEM((CH, RG, 512), BF16),
            dma((8,)), dma((6,)), dma((6,)), dma((CH, 8)), dma((CH, 8)),
            dma((4, 4)), dma((8, 4)), dma((4, 4)),
            dma((items, 4)), dma((CH, 8)),
            dma((CH, 2, 5)), dma((CH, 8, 2)), dma((CH, 4)), dma((CH, 2)), dma((CH, 2)),
            dma((2,)), dma((2,)),
        ],
        compiler_params=pltpu.CompilerParams(
            collective_id=0, has_side_effects=True, vmem_limit_bytes=60 * 2**20
        ),
        cost_estimate=pl.CostEstimate(
            flops=11_000_000_000, bytes_accessed=4_000_000, transcendentals=18_000_000
        ),
    )(queries, cache_keys, cache_values, new_keys, new_values, out_weight)


def solution(mesh):
    placed = (
        P("seq", "head"),
        P("seq", None),
        P("seq", None),
        P("seq", None),
        P("seq", None),
        P("seq", "head"),
    )
    return jax.shard_map(
        local, mesh=mesh, in_specs=placed, out_specs=P("seq", "head"), check_vma=False
    )
```

time: 113 us -> 83 us (0.73)
  the two profiles are of different devices: /device:TPU:6 before, /device:TPU:1 now
where the time goes in v3:
time: 83 us; the launch traced here: 82.9 us
  Pallas kernels  81.3 us (98%)
  local copies, waits for them, and re-layouts  1.57 us (2%)
    pallas_call x1, Pallas kernels, local(): pl.pallas_call(kernel, out_shape=jax.ShapeDtypeStruct((128, 512), BF16),...  81.3 us

profile of v3, /device:TPU:1, one launch (start us, length us, event | category | flops | bytes accessed | tf_op | source)
XLA Modules:
  0.0 82.9 jit_solution(5956352736929499585)
XLA Ops:
  0.0 81.3 %shard_map.64 = bf16[128,512]{1,0:T(8,128)(2,1)} custom-call(bf16[128,512]{1,0:T(8,128)(2,1)} %q_ref.1, bf16[2048,1024]{1,0:T(8,128)(2,1)} %ck_ref.1, bf16[2048,1024]{1,0:T(8,128)(2,1)} %cv_ref.1, bf16[128,1024]{1,0:T(8,128)(2,1)} %nk_ref.1, bf16[128,1024]{1,0:T(8,128)(2,1)} %nv_ref.1, bf16[512,512]{1,0:T(8,128)(2,1)} %w_ref.1), custom_call_target="tpu_custom_call" | custom-call | flops 11000000512 | bytes 4000000 | tf_op jit(solution)/shard_map/pallas_call | solution.py:464
  81.3 1.6 %copy.8 = bf16[128,512]{1,0:T(8,128)(2,1)} copy(bf16[128,512]{1,0:T(8,128)(2,1)} %shard_map.64) | data formatting | bytes 262144

commit v4 on v3

--- a/solution.py
+++ b/solution.py
@@ -54,7 +54,7 @@
     q_ref, ck_ref, cv_ref, nk_ref, nv_ref, w_ref, out_ref,
     k2, vraw, vt, sbuf, qbuf, qt, osend, obuf, amine, abuf, wbuf, acc, csend, cbuf,
     loc_sem, kv_send, kv_recv, q_send, q_recv, w_send, w_recv, wf_send,
-    o_send, o_recv, m_send, m_recv, z_send, z_recv, h_recv, c_send, c_recv,
+    o_send, o_recv, m_send, m_recv, z_send, z_recv, c_send, c_recv,
 ):
     s = lax.axis_index("seq")
     h = lax.axis_index("head")
@@ -115,14 +115,14 @@
     greet(partner)
     for d in (1, 2, 6, 7):
         greet((s, yh * 8 + (z + d) % 8))
-        for a in range(2):
-            greet((seq_of(a, x), yl * 8 + (z + d) % 8))
+    for a in range(2):
+        greet((seq_of(a, x), yl * 8 + (z + 4) % 8))
     for a in range(2):
         @pl.when(jnp.logical_or(yl != yh, yl != a))
         def _():
             greet((seq_of(a, x), yl * 8 + z))
 
-    pl.semaphore_wait(barrier, jnp.where(yl == yh, 21, 22))
+    pl.semaphore_wait(barrier, jnp.where(yl == yh, 15, 16))
 
     kv_out = [
         remote(src, dst, kv_send.at[n], kv_recv.at[n], partner)
@@ -155,8 +155,16 @@
         )
 
     def w_start(j):
-        for d in (1, 3, 2):
-            w_copy(d, j).start()
+        w_copy(1, j).start()
+        w_copy(3, j).start()
+
+    def w_on(j):
+        step = 1 + 2 * (j % 2)
+        slot = ((x + 4 - step) % 4) * 2 + c
+        ref = wbuf.at[slot, w_rows(j)]
+        return remote(
+            ref, ref, w_send.at[2, j], w_recv.at[slot, j], (seq_of(yl, (x + step) % 4), h)
+        )
 
     def w_forward(d):
         return remote(w_ref, wbuf.at[my_w], wf_send.at[0, 0], w_recv.at[my_w, 0], partner)
@@ -166,11 +174,26 @@
         ref = wbuf.at[slot, w_rows(j)]
         return remote(ref, ref, wf_send.at[d, j], w_recv.at[slot, j], partner)
 
-    def w_hand_on(j):
+    def w_far(d, j):
+        slot = ((x + 4 - d) % 4) * 2 + c
+        arrived(wbuf.at[slot, w_rows(j)], w_recv.at[slot, j])
+
+    def w_hand_on(j, last=False):
+        w_far(1, j)
+        w_far(3, j)
+        if not last:
+            w_on(j).start()
+        w_pass(1, j).start()
+        w_pass(3, j).start()
+
+    def w_hand_far(j):
+        w_far(2, j)
+        w_pass(2, j).start()
+
+    def w_partner(j):
         for d in (1, 3, 2):
-            slot = ((x + 4 - d) % 4) * 2 + c
+            slot = ((x + 4 - d) % 4) * 2 + 1 - c
             arrived(wbuf.at[slot, w_rows(j)], w_recv.at[slot, j])
-            w_pass(d, j).start()
 
     def flip(rows):
         vt[pl.ds(0, HD), rows] = vraw[rows, :].T
@@ -214,10 +237,10 @@
     def zz(d):
         return (z + 8 + d) % 8
 
-    def m_copy(g, a, d):
+    def m_copy(g, a, far):
         return remote(
-            amine.at[g], abuf.at[z, g, yl], m_send.at[g, a, d + 2], m_recv.at[g, z, yl],
-            (seq_of(yh, x), a * 8 + zz(d)),
+            amine.at[g], abuf.at[z, g, yl], m_send.at[g, a, far], m_recv.at[g, far, yl],
+            (seq_of(yh, x), a * 8 + zz(4 * far)),
         )
 
     def m_is_self(a):
@@ -230,45 +253,35 @@
         turned = result.T.astype(BF16)
         for n in range(G):
             amine[g, :, pl.ds(n * HD, HD)] = turned[n * RG : (n + 1) * RG]
-        for d in (-2, 2, -1, 1):
-            for a in range(2):
-                m_copy(g, a, d).start()
+        for a in range(2):
+            m_copy(g, a, 1).start()
         for a in range(2):
             @pl.when(m_is_self(a))
             def _():
-                pltpu.make_async_copy(amine.at[g], abuf.at[z, g, yl], m_recv.at[g, z, yl]).start()
+                pltpu.make_async_copy(amine.at[g], abuf.at[z, g, yl], m_recv.at[g, 0, yl]).start()
 
             @pl.when(jnp.logical_not(m_is_self(a)))
             def _():
                 m_copy(g, a, 0).start()
 
-    def m_wait(g, d):
+    def z_copies(g):
+        near, far = abuf.at[z, g], abuf.at[zz(4), g]
+        plan = ((near, 2), (near, -2), (far, 1), (far, -1), (near, 1), (near, -1))
+        return [
+            remote(ref, ref, z_send.at[g, n], z_recv.at[g, n], (s, yh * 8 + zz(d)))
+            for n, (ref, d) in enumerate(plan)
+        ]
+
+    def stage_z(g):
         for a in range(2):
-            arrived(abuf.at[zz(d), g, a], m_recv.at[g, zz(d), a])
-
-    def z_copies(g):
-        near, far = abuf.at[zz(-2), g], abuf.at[zz(2), g]
-        half, other = abuf.at[zz(-2), g, 0], abuf.at[zz(2), g, 1]
-        return (
-            remote(half, half, z_send.at[g, 0], h_recv.at[g, 0], (s, yh * 8 + zz(2))),
-            remote(other, other, z_send.at[g, 1], h_recv.at[g, 1], (s, yh * 8 + zz(-2))),
-            remote(near, near, z_send.at[g, 2], z_recv.at[g, 0], (s, yh * 8 + zz(1))),
-            remote(far, far, z_send.at[g, 3], z_recv.at[g, 1], (s, yh * 8 + zz(-1))),
-        )
-
-    def stage_z(g):
-        m_wait(g, -2)
-        m_wait(g, 2)
+            arrived(abuf.at[z, g, a], m_recv.at[g, 0, a])
+            arrived(abuf.at[zz(4), g, a], m_recv.at[g, 1, a])
         for copy in z_copies(g):
             copy.start()
 
     def z_wait(g):
-        for d in (-1, 0, 1):
-            m_wait(g, d)
-        arrived(abuf.at[zz(-3), g], z_recv.at[g, 0])
-        arrived(abuf.at[zz(3), g], z_recv.at[g, 1])
-        for a in range(2):
-            arrived(abuf.at[zz(4), g, a], h_recv.at[g, a])
+        for n, d in enumerate((-2, 2, 3, -3, -1, 1)):
+            arrived(abuf.at[zz(d), g], z_recv.at[g, n])
 
     def one_item(i, unused):
         g, sub = i // 2, i % 2
@@ -354,45 +367,86 @@
         def _():
             w_forward(0).start()
 
-        @pl.when(jnp.logical_and(sub == 1, i < 6))
+        @pl.when(jnp.logical_and(sub == 0, i < 6))
         def _():
             w_start(i // 2)
 
-        @pl.when(jnp.logical_and(sub == 0, i >= 4))
-        def _():
-            w_hand_on((i - 4) // 2)
+        @pl.when(jnp.logical_and(sub == 1, i >= 3))
+        def _():
+            w_hand_on((i - 3) // 2)
+
+        @pl.when(jnp.logical_and(sub == 1, i >= 5))
+        def _():
+            w_hand_far((i - 5) // 2)
 
         return unused
 
     lax.fori_loop(0, 2 * CH, one_item, 0)
+
+    def multiply(first, count, place, low, high):
+        rows = 2 * RG * count
+        block = abuf[place, first : first + count].reshape(rows, 512)
+        product = jnp.dot(
+            block[:, low:high], wbuf[place, pl.ds(low, high - low), :], preferred_element_type=F32
+        )
+        acc[first : first + count] += product.reshape(count, 2, RG, 512)
 
     stage_m(CH - 1)
     w_start(3)
+    w_copy(2, 3).start()
     stage_z(CH - 2)
-    w_hand_on(2)
-    stage_z(CH - 1)
-    w_hand_on(3)
-    for g in range(CH - 1):
+    w_hand_far(2)
+    acc[...] = jnp.zeros_like(acc)
+
+    def drain_item(i, unused):
+        for n in range(1, 4):
+            o_copy(i, n).wait_send()
+
+        @pl.when(i % 2 == 1)
+        def _():
+            o_copy(i, 0).wait_send()
+
+        return unused
+
+    lax.fori_loop(0, 2 * CH, drain_item, 0)
+    for g in range(CH - 2):
         z_wait(g)
     slot = my_w + 1 - 2 * c
     arrived(wbuf.at[slot], w_recv.at[slot, 0])
-    for j in range(4):
-        for d in (1, 3, 2):
-            slot = ((x + 4 - d) % 4) * 2 + 1 - c
-            arrived(wbuf.at[slot, w_rows(j)], w_recv.at[slot, j])
-
-    def multiply(first, count, place):
-        rows = 2 * RG * count
-        block = abuf[place, first : first + count].reshape(rows, COLS)
-        return jnp.dot(block, wbuf[place], preferred_element_type=F32).reshape(count, 2, RG, 512)
-
-    acc[...] = jnp.zeros_like(acc)
-
-    def early(place, unused):
-        acc[0 : CH - 1] += multiply(0, CH - 1, place)
+    for j in range(3):
+        w_partner(j)
+
+    def first_part(place, unused):
+        multiply(0, CH - 2, place, 0, 384)
         return unused
 
-    lax.fori_loop(0, 8, early, 0)
+    lax.fori_loop(0, 8, first_part, 0)
+    stage_z(CH - 1)
+    w_hand_on(3, last=True)
+    w_hand_far(3)
+
+    def drain_chunk(g, unused):
+        for n in range(1, 8):
+            q_copy(g, n).wait_send()
+        for a in range(2):
+            m_copy(g, a, 1).wait_send()
+
+            @pl.when(jnp.logical_not(m_is_self(a)))
+            def _():
+                m_copy(g, a, 0).wait_send()
+
+        return unused
+
+    lax.fori_loop(0, CH, drain_chunk, 0)
+    z_wait(CH - 2)
+    w_partner(3)
+
+    def second_part(place, unused):
+        multiply(0, CH - 2, place, 384, 512)
+        multiply(CH - 2, 1, place, 0, 512)
+        return unused
+
+    lax.fori_loop(0, 8, second_part, 0)
     for g in range(CH - 1):
         csend[g] = acc[g, 1 - yl].astype(BF16)
 
@@ -402,12 +456,26 @@
 
     swap(0).start()
 
-    def late(d):
-        acc[CH - 1 :] += multiply(CH - 1, 1, zz(d))
+    for copy in kv_out:
+        copy.wait_send()
+    w_forward(0).wait_send()
+    for j in range(4):
+        for d in range(1, 4):
+            if d == 2 and j < 3:
+                w_on(j).wait_send()
+            else:
+                w_copy(d, j).wait_send()
+            w_pass(d, j).wait_send()
+    for g in range(CH - 1):
+        for copy in z_copies(g):
+            copy.wait_send()
+
+    def last_part(place, unused):
+        multiply(CH - 1, 1, place, 0, 512)
+        return unused
 
     z_wait(CH - 1)
-    for d in range(8):
-        late(d - 4)
+    lax.fori_loop(0, 8, last_part, 0)
     csend[CH - 1] = acc[CH - 1, 1 - yl].astype(BF16)
     swap(1).start()
     swap(0).wait_recv()
@@ -418,42 +486,8 @@
 
     for n in range(2):
         swap(n).wait_send()
-    for copy in kv_out:
+    for copy in z_copies(CH - 1):
         copy.wait_send()
-    w_forward(0).wait_send()
-    for d in range(1, 4):
-        for j in range(4):
-            w_copy(d, j).wait_send()
-            w_pass(d, j).wait_send()
-
-    def drain_chunk(g, unused):
-        for n in range(1, 8):
-            q_copy(g, n).wait_send()
-        for a in range(2):
-            for d in (-2, -1, 1, 2):
-                m_copy(g, a, d).wait_send()
-
-            @pl.when(jnp.logical_not(m_is_self(a)))
-            def _():
-                m_copy(g, a, 0).wait_send()
-
-        for copy in z_copies(g):
-            copy.wait_send()
-        return unused
-
-    lax.fori_loop(0, CH, drain_chunk, 0)
-
-    def drain_item(i, unused):
-        for n in range(1, 4):
-            o_copy(i, n).wait_send()
-
-        @pl.when(i % 2 == 1)
-        def _():
-            o_copy(i, 0).wait_send()
-
-        return unused
-
-    lax.fori_loop(0, 2 * CH, drain_item, 0)
 
 
 def local(queries, cache_keys, cache_values, new_keys, new_values, out_weight):
@@ -484,7 +518,7 @@
             dma((8,)), dma((6,)), dma((6,)), dma((CH, 8)), dma((CH, 8)),
             dma((4, 4)), dma((8, 4)), dma((4, 4)),
             dma((items, 4)), dma((CH, 8)),
-            dma((CH, 2, 5)), dma((CH, 8, 2)), dma((CH, 4)), dma((CH, 2)), dma((CH, 2)),
+            dma((CH, 2, 2)), dma((CH, 2, 2)), dma((CH, 6)), dma((CH, 6)),
             dma((2,)), dma((2,)),
         ],
         compiler_params=pltpu.CompilerParams(

time: 83 us -> 78.8 us (0.949)
  the two profiles are of different devices: /device:TPU:1 before, /device:TPU:6 now
where the time goes in v4:
time: 78.8 us; the launch traced here: 78.7 us
  Pallas kernels  77.1 us (98%)
  local copies, waits for them, and re-layouts  1.57 us (2%)
    pallas_call x1, Pallas kernels, local(): pl.pallas_call(kernel, out_shape=jax.ShapeDtypeStruct((128, 512), BF16),...  77.1 us

profile of v4, /device:TPU:6, one launch (start us, length us, event | category | flops | bytes accessed | tf_op | source)
XLA Modules:
  0.0 78.7 jit_solution(16350495563487334984)
XLA Ops:
  0.0 77.1 %shard_map.64 = bf16[128,512]{1,0:T(8,128)(2,1)} custom-call(bf16[128,512]{1,0:T(8,128)(2,1)} %q_ref.1, bf16[2048,1024]{1,0:T(8,128)(2,1)} %ck_ref.1, bf16[2048,1024]{1,0:T(8,128)(2,1)} %cv_ref.1, bf16[128,1024]{1,0:T(8,128)(2,1)} %nk_ref.1, bf16[128,1024]{1,0:T(8,128)(2,1)} %nv_ref.1, bf16[512,512]{1,0:T(8,128)(2,1)} %w_ref.1), custom_call_target="tpu_custom_call" | custom-call | flops 11000000512 | bytes 4000000 | tf_op jit(solution)/shard_map/pallas_call | solution.py:498
  77.1 1.6 %copy.8 = bf16[128,512]{1,0:T(8,128)(2,1)} copy(bf16[128,512]{1,0:T(8,128)(2,1)} %shard_map.64) | data formatting | bytes 262144

commit v5 on v4

--- a/solution.py
+++ b/solution.py
@@ -52,7 +52,7 @@
 
 def kernel(
     q_ref, ck_ref, cv_ref, nk_ref, nv_ref, w_ref, out_ref,
-    k2, vraw, vt, sbuf, qbuf, qt, osend, obuf, amine, abuf, wbuf, acc, csend, cbuf,
+    keys, vraw, vt, sbuf, qbuf, qt, osend, obuf, amine, abuf, wbuf, acc, csend, cbuf,
     loc_sem, kv_send, kv_recv, q_send, q_recv, w_send, w_recv, wf_send,
     o_send, o_recv, m_send, m_recv, z_send, z_recv, c_send, c_recv,
 ):
@@ -86,10 +86,8 @@
 
     def kv_parts(core):
         return [
-            (ck_ref.at[:, kv_col], k2.at[cached_rows(core), pl.ds(0, HD)]),
-            (ck_ref.at[:, kv_col], k2.at[cached_rows(core), pl.ds(HD, HD)]),
-            (nk_ref.at[:, kv_col], k2.at[new_rows(core), pl.ds(0, HD)]),
-            (nk_ref.at[:, kv_col], k2.at[new_rows(core), pl.ds(HD, HD)]),
+            (ck_ref.at[:, kv_col], keys.at[cached_rows(core), :]),
+            (nk_ref.at[:, kv_col], keys.at[new_rows(core), :]),
             (cv_ref.at[:, kv_col], vraw.at[cached_rows(core), :]),
             (nv_ref.at[:, kv_col], vraw.at[new_rows(core), :]),
         ]
@@ -276,12 +274,17 @@
         for a in range(2):
             arrived(abuf.at[z, g, a], m_recv.at[g, 0, a])
             arrived(abuf.at[zz(4), g, a], m_recv.at[g, 1, a])
-        for copy in z_copies(g):
-            copy.start()
+        copies = z_copies(g)
+        for n in (4, 5, 0, 1, 2, 3):
+            copies[n].start()
+
+    def z_take(g, n):
+        d = (-2, 2, 3, -3, -1, 1)[n]
+        arrived(abuf.at[zz(d), g], z_recv.at[g, n])
 
     def z_wait(g):
-        for n, d in enumerate((-2, 2, 3, -3, -1, 1)):
-            arrived(abuf.at[zz(d), g], z_recv.at[g, n])
+        for n in range(6):
+            z_take(g, n)
 
     def one_item(i, unused):
         g, sub = i // 2, i % 2
@@ -303,13 +306,10 @@
         tall = jnp.concatenate(
             [qbuf[a * 4 + b, rows, pl.ds(n * HD, HD)] for a, b in places for n in range(G)], axis=0
         )
-        wide = tall.astype(F32).T * SCALE
-        high = wide.astype(BF16)
-        qt[pl.ds(0, HD), :] = high
-        qt[pl.ds(HD, HD), :] = (wide - high.astype(F32)).astype(BF16)
+        qt[...] = tall.T
 
         def score(rows):
-            return jnp.dot(k2[rows, :], qt[...], preferred_element_type=F32)
+            return jnp.dot(keys[rows, :], qt[...], preferred_element_type=F32) * SCALE
 
         def highest(top, scores):
             return jnp.maximum(top, jnp.max(scores.reshape(TK // 8, 8, COLS), axis=0))
@@ -324,7 +324,7 @@
             if core is c:
                 @pl.when(i == 0)
                 def _():
-                    for copy in kv_out[:4]:
+                    for copy in kv_out[:2]:
                         copy.wait_recv()
 
         col = lax.broadcasted_iota(jnp.int32, (1, COLS), 1)
@@ -340,7 +340,7 @@
 
         @pl.when(i == 0)
         def _():
-            for copy in kv_out[4:]:
+            for copy in kv_out[2:]:
                 copy.wait_recv()
             flip_cached(1 - c)
             flip(pl.ds(CACHED, 256))
@@ -474,10 +474,15 @@
         multiply(CH - 1, 1, place, 0, 512)
         return unused
 
-    z_wait(CH - 1)
-    lax.fori_loop(0, 8, last_part, 0)
+    last_part(z, 0)
+    last_part(zz(4), 0)
+    for n, d in ((4, -1), (5, 1), (0, -2), (1, 2), (2, 3), (3, -3)):
+        z_take(CH - 1, n)
+        last_part(zz(d), 0)
     csend[CH - 1] = acc[CH - 1, 1 - yl].astype(BF16)
     swap(1).start()
+    for copy in z_copies(CH - 1):
+        copy.wait_send()
     swap(0).wait_recv()
     for g in range(CH):
         if g == CH - 1:
@@ -486,8 +491,6 @@
 
     for n in range(2):
         swap(n).wait_send()
-    for copy in z_copies(CH - 1):
-        copy.wait_send()
 
 
 def local(queries, cache_keys, cache_values, new_keys, new_values, out_weight):
@@ -501,12 +504,12 @@
         in_specs=[vmem, hbm, hbm, hbm, hbm, hbm],
         out_specs=vmem,
         scratch_shapes=[
-            pltpu.VMEM((KEYS, 2 * HD), BF16),
+            pltpu.VMEM((KEYS, HD), BF16),
             pltpu.VMEM((KEYS, HD), BF16),
             pltpu.VMEM((VR, KEYS), BF16),
             pltpu.VMEM((KEYS, COLS), F32),
             pltpu.VMEM((8, 128, 512), BF16),
-            pltpu.VMEM((2 * HD, COLS), BF16),
+            pltpu.VMEM((HD, COLS), BF16),
             pltpu.VMEM((items, 4, VR, HD), BF16),
             pltpu.VMEM((CH, 8, VR, HD), BF16),
             pltpu.VMEM((CH, RG, 512), BF16),
@@ -515,7 +518,7 @@
             pltpu.VMEM((CH, 2, RG, 512), F32),
             pltpu.VMEM((CH, RG, 512), BF16),
             pltpu.VMEM((CH, RG, 512), BF16),
-            dma((8,)), dma((6,)), dma((6,)), dma((CH, 8)), dma((CH, 8)),
+            dma((8,)), dma((4,)), dma((4,)), dma((CH, 8)), dma((CH, 8)),
             dma((4, 4)), dma((8, 4)), dma((4, 4)),
             dma((items, 4)), dma((CH, 8)),
             dma((CH, 2, 2)), dma((CH, 2, 2)), dma((CH, 6)), dma((CH, 6)),

time: 78.8 us -> 77.3 us (0.981)
  Pallas kernels: 77.1 us -> 75.6 us
    pallas_call x1, Pallas kernels: 77.1 us -> 75.6 us  [local(): pl.pallas_call(kernel, out_shape=jax.ShapeDtypeStruct((128, 512), BF16),...]
where the time goes in v5:
time: 77.3 us; the launch traced here: 77.2 us
  Pallas kernels  75.6 us (98%)
  local copies, waits for them, and re-layouts  1.57 us (2%)
    pallas_call x1, Pallas kernels, local(): pl.pallas_call(kernel, out_shape=jax.ShapeDtypeStruct((128, 512), BF16),...  75.6 us
    unnamed x1, local copies, waits for them, and re-layouts  1.57 us

profile of v5, /device:TPU:6, one launch (start us, length us, event | category | flops | bytes accessed | tf_op | source)
XLA Modules:
  0.0 77.2 jit_solution(6420178780971159318)
XLA Ops:
  0.0 75.6 %shard_map.64 = bf16[128,512]{1,0:T(8,128)(2,1)} custom-call(bf16[128,512]{1,0:T(8,128)(2,1)} %q_ref.1, bf16[2048,1024]{1,0:T(8,128)(2,1)} %ck_ref.1, bf16[2048,1024]{1,0:T(8,128)(2,1)} %cv_ref.1, bf16[128,1024]{1,0:T(8,128)(2,1)} %nk_ref.1, bf16[128,1024]{1,0:T(8,128)(2,1)} %nv_ref.1, bf16[512,512]{1,0:T(8,128)(2,1)} %w_ref.1), custom_call_target="tpu_custom_call" | custom-call | flops 11000000512 | bytes 4000000 | tf_op jit(solution)/shard_map/pallas_call | solution.py:501
  75.6 1.6 %copy.8 = bf16[128,512]{1,0:T(8,128)(2,1)} copy(bf16[128,512]{1,0:T(8,128)(2,1)} %shard_map.64) | data formatting | bytes 262144

commit v6 on v5

--- a/solution.py
+++ b/solution.py
@@ -409,19 +409,18 @@
         return unused
 
     lax.fori_loop(0, 2 * CH, drain_item, 0)
+    def first_part(place, unused):
+        multiply(0, CH - 2, place, 0, 384)
+        return unused
+
+    stage_z(CH - 1)
     for g in range(CH - 2):
         z_wait(g)
     slot = my_w + 1 - 2 * c
     arrived(wbuf.at[slot], w_recv.at[slot, 0])
     for j in range(3):
         w_partner(j)
-
-    def first_part(place, unused):
-        multiply(0, CH - 2, place, 0, 384)
-        return unused
-
     lax.fori_loop(0, 8, first_part, 0)
-    stage_z(CH - 1)
     w_hand_on(3, last=True)
     w_hand_far(3)
 
@@ -456,6 +455,17 @@
 
     swap(0).start()
 
+    def last_part(place, unused):
+        multiply(CH - 1, 1, place, 0, 512)
+        return unused
+
+    last_part(z, 0)
+    last_part(zz(4), 0)
+    for n, d in ((4, -1), (5, 1), (0, -2), (1, 2), (2, 3), (3, -3)):
+        z_take(CH - 1, n)
+        last_part(zz(d), 0)
+    csend[CH - 1] = acc[CH - 1, 1 - yl].astype(BF16)
+    swap(1).start()
     for copy in kv_out:
         copy.wait_send()
     w_forward(0).wait_send()
@@ -469,18 +479,6 @@
     for g in range(CH - 1):
         for copy in z_copies(g):
             copy.wait_send()
-
-    def last_part(place, unused):
-        multiply(CH - 1, 1, place, 0, 512)
-        return unused
-
-    last_part(z, 0)
-    last_part(zz(4), 0)
-    for n, d in ((4, -1), (5, 1), (0, -2), (1, 2), (2, 3), (3, -3)):
-        z_take(CH - 1, n)
-        last_part(zz(d), 0)
-    csend[CH - 1] = acc[CH - 1, 1 - yl].astype(BF16)
-    swap(1).start()
     for copy in z_copies(CH - 1):
         copy.wait_send()
     swap(0).wait_recv()

time: 77.3 us -> 78.2 us (1.012); the launches traced: 77.2 us -> 77.2 us
  no operation moved by 1% of the time
where the time goes in v6:
time: 78.2 us; the launch traced here: 77.2 us
  Pallas kernels  75.7 us (97%)
  local copies, waits for them, and re-layouts  1.57 us (2%)
    pallas_call x1, Pallas kernels, local(): pl.pallas_call(kernel, out_shape=jax.ShapeDtypeStruct((128, 512), BF16),...  75.7 us
    unnamed x1, local copies, waits for them, and re-layouts  1.57 us

profile of v6, /device:TPU:6, one launch (start us, length us, event | category | flops | bytes accessed | tf_op | source)
XLA Modules:
  0.0 77.2 jit_solution(7861106031571322646)
XLA Ops:
  0.0 75.7 %shard_map.64 = bf16[128,512]{1,0:T(8,128)(2,1)} custom-call(bf16[128,512]{1,0:T(8,128)(2,1)} %q_ref.1, bf16[2048,1024]{1,0:T(8,128)(2,1)} %ck_ref.1, bf16[2048,1024]{1,0:T(8,128)(2,1)} %cv_ref.1, bf16[128,1024]{1,0:T(8,128)(2,1)} %nk_ref.1, bf16[128,1024]{1,0:T(8,128)(2,1)} %nv_ref.1, bf16[512,512]{1,0:T(8,128)(2,1)} %w_ref.1), custom_call_target="tpu_custom_call" | custom-call | flops 11000000512 | bytes 4000000 | tf_op jit(solution)/shard_map/pallas_call | solution.py:499
  75.7 1.6 %copy.8 = bf16[128,512]{1,0:T(8,128)(2,1)} copy(bf16[128,512]{1,0:T(8,128)(2,1)} %shard_map.64) | data formatting | bytes 262144

commit v7 on v6

--- a/solution.py
+++ b/solution.py
@@ -409,18 +409,19 @@
         return unused
 
     lax.fori_loop(0, 2 * CH, drain_item, 0)
-    def first_part(place, unused):
-        multiply(0, CH - 2, place, 0, 384)
-        return unused
-
-    stage_z(CH - 1)
     for g in range(CH - 2):
         z_wait(g)
     slot = my_w + 1 - 2 * c
     arrived(wbuf.at[slot], w_recv.at[slot, 0])
     for j in range(3):
         w_partner(j)
+
+    def first_part(place, unused):
+        multiply(0, CH - 2, place, 0, 384)
+        return unused
+
     lax.fori_loop(0, 8, first_part, 0)
+    stage_z(CH - 1)
     w_hand_on(3, last=True)
     w_hand_far(3)
 

time: 78.2 us -> 77.3 us (0.988); the launches traced: 77.2 us -> 77.2 us
  no operation moved by 1% of the time
where the time goes in v7:
time: 77.3 us; the launch traced here: 77.2 us
  Pallas kernels  75.6 us (98%)
  local copies, waits for them, and re-layouts  1.57 us (2%)
    pallas_call x1, Pallas kernels, local(): pl.pallas_call(kernel, out_shape=jax.ShapeDtypeStruct((128, 512), BF16),...  75.6 us
    unnamed x1, local copies, waits for them, and re-layouts  1.57 us

profile of v7, /device:TPU:6, one launch (start us, length us, event | category | flops | bytes accessed | tf_op | source)
XLA Modules:
  0.0 77.2 jit_solution(5774981120448910670)
XLA Ops:
  0.0 75.6 %shard_map.64 = bf16[128,512]{1,0:T(8,128)(2,1)} custom-call(bf16[128,512]{1,0:T(8,128)(2,1)} %q_ref.1, bf16[2048,1024]{1,0:T(8,128)(2,1)} %ck_ref.1, bf16[2048,1024]{1,0:T(8,128)(2,1)} %cv_ref.1, bf16[128,1024]{1,0:T(8,128)(2,1)} %nk_ref.1, bf16[128,1024]{1,0:T(8,128)(2,1)} %nv_ref.1, bf16[512,512]{1,0:T(8,128)(2,1)} %w_ref.1), custom_call_target="tpu_custom_call" | custom-call | flops 11000000512 | bytes 4000000 | tf_op jit(solution)/shard_map/pallas_call | solution.py:500
  75.6 1.6 %copy.8 = bf16[128,512]{1,0:T(8,128)(2,1)} copy(bf16[128,512]{1,0:T(8,128)(2,1)} %shard_map.64) | data formatting | bytes 262144
